TPU v7x, 32 devices: a whole 2x2x4 slice. The times are simulated.
32 devices in a mesh: grp: 2 (over x), fsdp: 16 (over z, y, core).
Axes of the slice: x: 2, y: 2, z: 4, core: 2. Of those that a mesh axis runs over, the one named last changes fastest.
Arguments:
- inputs: bfloat16 [2, 2048, 1536], P('grp', 'fsdp'), may hold values from -6 to 6
- cotangent: bfloat16 [2, 2048, 1536], P('grp', 'fsdp'), may hold values from -6 to 6
- weights: float32 [1536, 19968], P(('grp', 'fsdp')), may hold values from -2.44948974 to 2.44948974
- weights_first: float32 [1536, 19968], P(('grp', 'fsdp')), may hold values from -0.00030517578 to 0.00030517578
- weights_second: float32 [1536, 19968], P(('grp', 'fsdp')), may hold values from 1.6279285e-09 to 6.511714e-09
- gains: float32 [4, 1536], replicated, may hold values from 0.8 to 6.25
- gains_first: float32 [4, 1536], replicated, may hold values from -0.00030517578 to 0.00030517578
- gains_second: float32 [4, 1536], replicated, may hold values from 1.6279285e-09 to 6.511714e-09
- forget_weight: float32 [1536, 24], replicated, may hold values from -0.078125 to 0.078125
- forget_first: float32 [1536, 24], replicated, may hold values from -0.00030517578 to 0.00030517578
- forget_second: float32 [1536, 24], replicated, may hold values from 1.6279285e-09 to 6.511714e-09
- forget_bias: float32 [24], replicated
- bias_first: float32 [24], replicated, may hold values from -0.00030517578 to 0.00030517578
- bias_second: float32 [24], replicated, may hold values from 1.6279285e-09 to 6.511714e-09
Outputs:
- output: bfloat16 [2, 2048, 1536], P('grp', 'fsdp')
- input_grad: bfloat16 [2, 2048, 1536], P('grp', 'fsdp')
- grad_norm: float32 [], replicated
- new_weights: float32 [1536, 19968], P(('grp', 'fsdp'))
- new_weights_first: float32 [1536, 19968], P(('grp', 'fsdp'))
- new_weights_second: float32 [1536, 19968], P(('grp', 'fsdp'))
- new_gains: float32 [4, 1536], replicated
- new_gains_first: float32 [4, 1536], replicated
- new_gains_second: float32 [4, 1536], replicated
- new_forget_weight: float32 [1536, 24], replicated
- new_forget_first: float32 [1536, 24], replicated
- new_forget_second: float32 [1536, 24], replicated
- new_forget_bias: float32 [24], replicated
- new_bias_first: float32 [24], replicated
- new_bias_second: float32 [24], replicated
All inputs are finite; a program needn't handle non-finite values.
Results may differ from a plain program's by a relative error of at most 0.038.
Values may be sent and summed in bfloat16 or wider, within the bound.
A program may use at most 640 MiB of HBM per device.

v0:
```python
import jax
import jax.numpy as jnp
from jax import lax
from jax.sharding import PartitionSpec as P

D = 1536
H = 24
DH = 64
F = 4096
STEP = 5


EPS = 1e-06
BETA_ONE = 0.9
BETA_TWO = 0.95
ADAM_EPS = 1e-08
RATE_MATRIX = 0.1
RATE_GAIN = 1.2
RATE_BIAS = 3.0
DECAY = 0.1
CLIP = 1.0
NEGATIVE = -1e30


def entering(value, axis, combine, identity):
    size, index = (lax.axis_size(axis), lax.axis_index(axis))
    everything = lax.all_gather(value, axis)
    start = jnp.broadcast_to(jnp.asarray(identity, value.dtype), value.shape)

    def hop(k, before):
        at = size - 1 - k
        reached = at > index
        new = combine(before, everything[at])
        return jnp.where(reached, new, before)

    return lax.fori_loop(0, size, hop, start)


def rms_rows(value, gain):
    return value * lax.rsqrt(jnp.mean(value * value, axis=-1, keepdims=True) + EPS) * gain


def head_norm(value, gain):
    count = value.shape[0]
    heads = value.reshape(count, H, DH)
    heads = heads * lax.rsqrt(jnp.mean(heads * heads, axis=-1, keepdims=True) + EPS)
    return heads.reshape(count, H * DH) * gain


def block_size(count):
    return max((step for step in range(1, min(count, 512) + 1) if count % step == 0))


def split_blocks(array, step):
    return array.reshape((array.shape[0] // step, step) + array.shape[1:])


def keep_state(state):
    return state


def add_arrays(earlier, later):
    return earlier + later


def fold_rows(piece, left):
    return jnp.dot(left, piece, preferred_element_type=jnp.float32)


def map_rows(piece, left):
    return jnp.einsum("tc,rc->tr", left, piece, preferred_element_type=jnp.float32)


def owner_order(left, groups, members, owned):
    tokens = left.shape[0]
    return (
        left.reshape(tokens, groups, members, owned)
        .transpose(0, 2, 1, 3)
        .reshape(tokens, groups * members * owned)
    )


def grad_terms(pairs):
    terms = []
    for left, right in pairs:
        terms.append(jnp.einsum("tr,tc->rc", left, right, preferred_element_type=jnp.float32))
    return jnp.concatenate(terms, axis=1)


def scores_of(query_block, key_block, query_sum, key_sum, query_start, key_start, scale):
    scores = (
        jnp.einsum("qhd,khd->hqk", query_block, key_block, preferred_element_type=jnp.float32)
        * scale
    )
    scores = scores + query_sum.T[:, :, None] - key_sum.T[:, None, :]
    query_pos = query_start + jnp.arange(query_block.shape[0], dtype=jnp.int32)
    key_pos = key_start + jnp.arange(key_block.shape[0], dtype=jnp.int32)
    return jnp.where((key_pos[None, :] <= query_pos[:, None])[None], scores, NEGATIVE)


def forward_keys(state, pieces, start, queries, query_sum, forget_all, my_start, scale):
    count = pieces[0].shape[0]
    step = block_size(count)
    key_blocks = split_blocks(pieces[0].reshape(count, H, DH), step)
    value_blocks = split_blocks(pieces[1].reshape(count, H, DH), step)
    starts = start + jnp.arange(count // step, dtype=jnp.int32) * step
    rows = queries.shape[0]

    def forward_visit(carry, block):
        key_block, value_block, block_start = block

        def work(inner):
            top, total, accum = inner
            key_sum = lax.dynamic_slice_in_dim(forget_all, block_start, step, 0)
            scores = scores_of(queries, key_block, query_sum, key_sum, my_start, block_start, scale)
            new_top = jnp.maximum(top, jnp.max(scores, axis=-1))
            shrink = jnp.exp(top - new_top)
            weight = jnp.exp(scores - new_top[:, :, None])
            total = total * shrink + jnp.sum(weight, axis=-1)
            accum = accum * shrink.T[:, :, None] + jnp.einsum(
                "hqk,khd->qhd",
                weight.astype(jnp.bfloat16),
                value_block,
                preferred_element_type=jnp.float32,
            )
            return (new_top, total, accum)

        return (lax.cond(block_start <= my_start + rows - 1, work, keep_state, carry), None)

    state, unused = lax.scan(forward_visit, state, (key_blocks, value_blocks, starts))
    return state


def backward_pieces(state, pieces, start, mine, stats, forget_all, my_start, scale):
    my_queries, my_keys, my_values, my_grads, my_sum, my_lse, my_delta = mine
    lse_all, delta_all = stats
    count = pieces[0].shape[0]
    step = block_size(count)
    blocks = tuple((split_blocks(piece.reshape(count, H, DH), step) for piece in pieces))
    starts = start + jnp.arange(count // step, dtype=jnp.int32) * step
    rows = my_queries.shape[0]

    def backward_visit(carry, block):
        key_block, value_block, query_block, grad_block, block_start = block

        def query_side(inner):
            grad_query, grad_key, grad_value, grad_sum = inner
            key_sum = lax.dynamic_slice_in_dim(forget_all, block_start, step, 0)
            scores = scores_of(my_queries, key_block, my_sum, key_sum, my_start, block_start, scale)
            prob = jnp.exp(scores - my_lse.T[:, :, None])
            dprob = jnp.einsum(
                "qhd,khd->hqk", my_grads, value_block, preferred_element_type=jnp.float32
            )
            dscore = prob * (dprob - my_delta.T[:, :, None])
            grad_query = grad_query + jnp.einsum(
                "hqk,khd->qhd",
                (dscore * scale).astype(jnp.bfloat16),
                key_block,
                preferred_element_type=jnp.float32,
            )
            return (grad_query, grad_key, grad_value, grad_sum + jnp.sum(dscore, axis=-1).T)

        def key_side(inner):
            grad_query, grad_key, grad_value, grad_sum = inner
            query_sum = lax.dynamic_slice_in_dim(forget_all, block_start, step, 0)
            lse_rows = lax.dynamic_slice_in_dim(lse_all, block_start, step, 0)
            delta_rows = lax.dynamic_slice_in_dim(delta_all, block_start, step, 0)
            scores = scores_of(
                query_block, my_keys, query_sum, my_sum, block_start, my_start, scale
            )
            prob = jnp.exp(scores - lse_rows.T[:, :, None])
            dprob = jnp.einsum(
                "qhd,khd->hqk", grad_block, my_values, preferred_element_type=jnp.float32
            )
            dscore = prob * (dprob - delta_rows.T[:, :, None])
            grad_key = grad_key + jnp.einsum(
                "hqk,qhd->khd",
                (dscore * scale).astype(jnp.bfloat16),
                query_block,
                preferred_element_type=jnp.float32,
            )
            grad_value = grad_value + jnp.einsum(
                "hqk,qhd->khd",
                prob.astype(jnp.bfloat16),
                grad_block,
                preferred_element_type=jnp.float32,
            )
            return (grad_query, grad_key, grad_value, grad_sum - jnp.sum(dscore, axis=1).T)

        carry = lax.cond(block_start <= my_start + rows - 1, query_side, keep_state, carry)
        carry = lax.cond(block_start + step - 1 >= my_start, key_side, keep_state, carry)
        return (carry, None)

    state, unused = lax.scan(backward_visit, state, blocks + (starts,))
    return state


def adam(value, first, second, grad, rate, decay):
    first = BETA_ONE * first + (1.0 - BETA_ONE) * grad
    second = BETA_TWO * second + (1.0 - BETA_TWO) * grad * grad
    unbiased_first = first / (1.0 - BETA_ONE**STEP)
    unbiased_second = second / (1.0 - BETA_TWO**STEP)
    value = value - rate * (unbiased_first / (jnp.sqrt(unbiased_second) + ADAM_EPS) + decay * value)
    return (value, first, second)


def shards(
    inputs,
    cotangent,
    weights,
    weights_first,
    weights_second,
    gains,
    gains_first,
    gains_second,
    forget_weight,
    forget_first,
    forget_second,
    forget_bias,
    bias_first,
    bias_second,
):
    floats = jnp.float32
    halves = jnp.bfloat16
    source = inputs[0].astype(floats)
    returned = cotangent[0]
    rows = source.shape[0]
    own_rows = weights.shape[0]
    scale = DH ** (-0.5)
    devices = lax.axis_size("fsdp")
    groups = lax.axis_size("grp")
    my_start = lax.axis_index("fsdp") * rows
    narrow = weights.astype(halves)
    forget_low = forget_weight.astype(halves)
    first_norm, first_pull = jax.vjp(rms_rows, source, gains[0])
    first = first_norm.astype(halves)
    projected = fold_rows(
        lax.all_gather(narrow[:, : 4 * D], ("grp", "fsdp"), axis=0, tiled=True), left=first
    )
    logit = jnp.dot(first, forget_low, preferred_element_type=floats) + forget_bias
    query_norm, query_pull = jax.vjp(head_norm, projected[:, :D], gains[2])
    key_norm, key_pull = jax.vjp(head_norm, projected[:, D : 2 * D], gains[3])
    queries = query_norm.astype(halves)
    keys = key_norm.astype(halves)
    values = projected[:, 2 * D : 3 * D].astype(halves)
    gate = jax.nn.sigmoid(projected[:, 3 * D :])
    local_sum = jnp.cumsum(jax.nn.log_sigmoid(logit), axis=0)
    gathered_sum = lax.all_gather(local_sum, "fsdp", axis=0, tiled=True).reshape(devices, rows, H)
    ends = gathered_sum[:, rows - 1]
    forget_all = (gathered_sum + (jnp.cumsum(ends, axis=0) - ends)[:, None]).reshape(
        devices * rows, H
    )
    my_sum = lax.dynamic_slice_in_dim(forget_all, my_start, rows, 0)
    query_heads = queries.reshape(rows, H, DH)
    start_state = (
        jnp.full((H, rows), NEGATIVE, floats),
        jnp.zeros((H, rows), floats),
        jnp.zeros((rows, H, DH), floats),
    )
    top, total, accum = forward_keys(
        start_state,
        (
            lax.all_gather(keys, "fsdp", axis=0, tiled=True),
            lax.all_gather(values, "fsdp", axis=0, tiled=True),
        ),
        jnp.int32(0),
        queries=query_heads,
        query_sum=my_sum,
        forget_all=forget_all,
        my_start=my_start,
        scale=scale,
    )
    attended = (accum / total.T[:, :, None]).reshape(rows, D)
    lse = (top + jnp.log(total)).T
    gated = (attended * gate).astype(halves)
    out_weight, down_weight = (
        lax.all_gather(narrow[:, 4 * D : 5 * D], ("grp", "fsdp"), axis=0, tiled=True),
        lax.all_gather(narrow[:, 5 * D + 2 * F :], ("grp", "fsdp"), axis=0, tiled=True),
    )
    mixed = source + jnp.einsum("ti,oi->to", gated, out_weight, preferred_element_type=floats)
    second_norm, second_pull = jax.vjp(rms_rows, mixed, gains[1])
    second = second_norm.astype(halves)
    gate_up = fold_rows(
        lax.all_gather(narrow[:, 5 * D : 5 * D + 2 * F], ("grp", "fsdp"), axis=0, tiled=True),
        left=second,
    )
    gate_part = gate_up[:, :F]
    up_part = gate_up[:, F:]
    swish = jax.nn.silu(gate_part)
    hidden = (swish * up_part).astype(halves)
    result = mixed + jnp.einsum("tf,of->to", hidden, down_weight, preferred_element_type=floats)
    output = result.astype(halves)[None]
    grad_hidden = jnp.dot(returned, down_weight, preferred_element_type=floats)
    sig = jax.nn.sigmoid(gate_part)
    grad_gate_up = jnp.concatenate(
        [grad_hidden * up_part * sig * (1.0 + gate_part * (1.0 - sig)), grad_hidden * swish], axis=1
    ).astype(halves)
    mlp_pairs = (
        (owner_order(second, groups, devices, own_rows), grad_gate_up),
        (owner_order(returned, groups, devices, own_rows), hidden),
    )
    grad_second = map_rows(
        lax.all_gather(narrow[:, 5 * D : 5 * D + 2 * F], ("grp", "fsdp"), axis=0, tiled=True),
        left=grad_gate_up,
    )
    grad_mixed_norm, grad_gain_mid = second_pull(grad_second)
    grad_mixed = returned.astype(floats) + grad_mixed_norm
    grad_branch = grad_mixed.astype(halves)
    grad_gated = jnp.dot(grad_branch, out_weight, preferred_element_type=floats)
    grad_attended = (grad_gated * gate).astype(halves)
    grad_gate_logit = grad_gated * attended * gate * (1.0 - gate)
    delta = jnp.sum((grad_attended.astype(floats) * attended).reshape(rows, H, DH), axis=-1)
    lse_all, delta_all = (
        lax.all_gather(lse, "fsdp", axis=0, tiled=True),
        lax.all_gather(delta, "fsdp", axis=0, tiled=True),
    )
    mine = (
        query_heads,
        keys.reshape(rows, H, DH),
        values.reshape(rows, H, DH),
        grad_attended.reshape(rows, H, DH),
        my_sum,
        lse,
        delta,
    )
    back_state = (
        jnp.zeros((rows, H, DH), floats),
        jnp.zeros((rows, H, DH), floats),
        jnp.zeros((rows, H, DH), floats),
        jnp.zeros((rows, H), floats),
    )
    grad_query, grad_key, grad_value, grad_sum = backward_pieces(
        back_state,
        (
            lax.all_gather(keys, "fsdp", axis=0, tiled=True),
            lax.all_gather(values, "fsdp", axis=0, tiled=True),
            lax.all_gather(queries, "fsdp", axis=0, tiled=True),
            lax.all_gather(grad_attended, "fsdp", axis=0, tiled=True),
        ),
        jnp.int32(0),
        mine=mine,
        stats=(lse_all, delta_all),
        forget_all=forget_all,
        my_start=my_start,
        scale=scale,
    )
    later = entering(jnp.sum(grad_sum, axis=0), "fsdp", add_arrays, jnp.zeros((H,), floats))
    grad_log = later + jnp.cumsum(grad_sum[::-1], axis=0)[::-1]
    grad_logit = (grad_log * jax.nn.sigmoid(-logit)).astype(halves)
    grad_query_raw, grad_gain_query = query_pull(grad_query.reshape(rows, D))
    grad_key_raw, grad_gain_key = key_pull(grad_key.reshape(rows, D))
    grad_projected = jnp.concatenate(
        [grad_query_raw, grad_key_raw, grad_value.reshape(rows, D), grad_gate_logit], axis=1
    ).astype(halves)
    grad_first = map_rows(
        lax.all_gather(narrow[:, : 4 * D], ("grp", "fsdp"), axis=0, tiled=True), left=grad_projected
    )
    grad_first = grad_first + jnp.einsum(
        "th,dh->td", grad_logit, forget_low, preferred_element_type=floats
    )
    grad_source_norm, grad_gain_in = first_pull(grad_first)
    input_grad = (grad_mixed + grad_source_norm).astype(halves)[None]
    grad_forget = jnp.einsum("td,th->dh", first, grad_logit, preferred_element_type=floats)
    grad_bias = jnp.sum(grad_logit.astype(floats), axis=0)
    attn_pairs = (
        (owner_order(first, groups, devices, own_rows), grad_projected),
        (owner_order(grad_branch, groups, devices, own_rows), gated),
    )
    member_grads = lax.psum_scatter(
        grad_terms(pairs=attn_pairs + mlp_pairs), "fsdp", scatter_dimension=0, tiled=True
    )
    grad_weights = lax.psum_scatter(
        member_grads.astype(jnp.bfloat16), "grp", scatter_dimension=0, tiled=True
    ).astype(jnp.float32)
    grad_gains = jnp.stack([grad_gain_in, grad_gain_mid, grad_gain_query, grad_gain_key])
    squares, grad_gains, grad_forget, grad_bias = lax.psum(
        (jnp.sum(grad_weights * grad_weights), grad_gains, grad_forget, grad_bias), ("grp", "fsdp")
    )
    grad_norm = jnp.sqrt(
        squares
        + jnp.sum(grad_gains * grad_gains)
        + jnp.sum(grad_forget * grad_forget)
        + jnp.sum(grad_bias * grad_bias)
    )
    factor = CLIP / jnp.maximum(grad_norm, CLIP)
    new_w, new_wf, new_ws = adam(
        weights, weights_first, weights_second, grad_weights * factor, RATE_MATRIX, DECAY
    )
    new_g, new_gf, new_gs = adam(
        gains, gains_first, gains_second, grad_gains * factor, RATE_GAIN, 0.0
    )
    new_fw, new_ff, new_fs = adam(
        forget_weight, forget_first, forget_second, grad_forget * factor, RATE_MATRIX, DECAY
    )
    new_fb, new_bf, new_bs = adam(
        forget_bias, bias_first, bias_second, grad_bias * factor, RATE_BIAS, 0.0
    )
    return (
        output,
        input_grad,
        grad_norm,
        new_w,
        new_wf,
        new_ws,
        new_g,
        new_gf,
        new_gs,
        new_fw,
        new_ff,
        new_fs,
        new_fb,
        new_bf,
        new_bs,
    )


def solution(mesh):
    placed = (
        P("grp", "fsdp", None),
        P("grp", "fsdp", None),
        P(("grp", "fsdp"), None),
        P(("grp", "fsdp"), None),
        P(("grp", "fsdp"), None),
        P(),
        P(),
        P(),
        P(),
        P(),
        P(),
        P(),
        P(),
        P(),
    )
    return jax.shard_map(
        shards,
        mesh=mesh,
        in_specs=placed,
        out_specs=(
            P("grp", "fsdp", None),
            P("grp", "fsdp", None),
            P(),
            P(("grp", "fsdp"), None),
            P(("grp", "fsdp"), None),
            P(("grp", "fsdp"), None),
            P(),
            P(),
            P(),
            P(),
            P(),
            P(),
            P(),
            P(),
            P(),
        ),
        check_vma=False,
    )
```

profile of v0, /device:TPU:0, one launch (start us, length us, event | category | flops | bytes accessed | tf_op | source)
XLA Modules:
  0.0 2364.4 jit_solution(15248510114524313944)
XLA Ops:
  13.6 125.6 %all-gather.10.cloned.1.call-done = bf16[1536,6144]{1,0:T(8,128)(2,1)} async-done(((bf16[48,6144]{1,0:T(8,128)(2,1)}), bf16[1536,6144]{1,0:T(8,128)(2,1)}) %all-gather.10.cloned.1.call-update) | async-done | bytes 18874384 | tf_op jit(solution)/shard_map/all_gather | solution.py:238
  139.2 7.9 fusion.132
  148.4 2.5 copy.68
  179.2 26.6 %all_gather.45 = f32[2048,24]{1,0:T(8,128)S(1)} all-gather(f32[128,24]{1,0:T(8,128)} %reduce_window_sum.28), channel_id=1, replica_groups=mesh['grp'=2,'fsdp'=16] {'fsdp'}, dimensions={0}, use_global_device_ids=true | all-gather | bytes 208896 | tf_op jit(solution)/shard_map/all_gather | solution.py:248
  214.0 16.1 all-gather.12.cloned.1.call-done
  230.1 16.3 reshape.374
  246.3 14.0 copy.73
  260.4 32.8 %all-gather.14.cloned.1.call-done = bf16[2048,1536]{1,0:T(8,128)(2,1)} async-done(((bf16[128,1536]{1,0:T(8,128)(2,1)}), bf16[2048,1536]{1,0:T(8,128)(2,1)}) %all-gather.14.cloned.1.call-update) | async-done | bytes 6291472 | tf_op jit(solution)/shard_map/all_gather | solution.py:264
  293.2 16.3 reshape.375
  309.4 14.0 copy.76
  325.0 20.5 while.53
  326.3 15.2 conditional.6
  330.1 4.1 fusion.2
  334.2 4.2 fusion.16
  352.0 6.7 all-gather.16.cloned.1.call-done
  358.7 4.2 multiply_reduce_fusion.6
  364.7 150.8 %all-gather.18.cloned.1.call-done = bf16[1536,8192]{1,0:T(8,128)(2,1)} async-done(((bf16[48,8192]{1,0:T(8,128)(2,1)}), bf16[1536,8192]{1,0:T(8,128)(2,1)}) %all-gather.18.cloned.1.call-update) | async-done | bytes 25165840 | tf_op jit(solution)/shard_map/all_gather | solution.py:284
  515.5 13.7 fusion.143
  529.2 83.2 %all-gather.20.cloned.1.call-done = bf16[1536,4096]{1,0:T(8,128)(2,1)} async-done(((bf16[48,4096]{1,0:T(8,128)(2,1)}), bf16[1536,4096]{1,0:T(8,128)(2,1)}) %all-gather.20.cloned.1.call-update) | async-done | bytes 12582928 | tf_op jit(solution)/shard_map/all_gather | solution.py:278
  612.4 10.5 multiply_convert_fusion.13
  622.9 15.3 multiply_reduce_fusion.2
  641.3 5.6 convert_multiply_fusion.2
  656.9 18.5 all-gather.22.cloned.1.call-done
  675.4 16.3 reshape.372
  691.7 14.1 copy.89
  706.5 21.9 all_gather.51
  731.0 18.2 all_gather.53
  749.3 5.0 fusion.144
  754.2 10.2 convolution_bitcast_fusion
  764.4 20.5 fusion.92
  784.9 16.3 reshape.373
  801.2 14.1 copy.90
  816.4 96.6 %while.54 = (s32[]{:T(128)}, f32[128,24,64]{0,2,1:T(8,128)S(1)}, f32[128,24,64]{0,2,1:T(8,128)S(1)}, f32[128,24,64]{0,2,1:T(8,128)}, f32[128,24]{0,1:T(8,128)S(1...) while((s32[]{:T(128)}, f32[128,24,64]{0,2,1:T(8,128)S(1)}, ...), condition=%wide.region_21.22_spmd, body=%wide.region_14.21_spmd.sunk | while | flops 1450902784 | bytes 109913520 | solution.py:194
  818.5 13.2 conditional.7
  824.0 5.4 fusion.140
  831.7 18.8 conditional.8
  838.6 3.8 fusion.73
  842.4 5.8 fusion.141
  852.5 18.8 conditional.8
  859.4 3.8 fusion.73
  863.2 5.8 fusion.141
  873.2 18.8 conditional.8
  877.6 2.5 fusion.56
  880.1 3.8 fusion.73
  883.9 5.8 fusion.141
  894.0 18.8 conditional.8
  900.9 3.8 fusion.73
  904.7 5.8 fusion.141
  920.2 2.6 fusion.95
  925.3 15.8 fusion.112
  941.1 80.2 %pad_maximum_fusion = f32[1536,19968]{1,0:T(8,128)} fusion(f32[1536,4096]{1,0:T(8,128)} %convolution_bitcast_fusion, f32[1536,8192]{1,0:T(8,128)} %fusion.92, f32[1536,1536]{1,0:T(8,128)} %fusion.144, f32[1536,6144]{1,0:T(8,128)} %fusion.112), kind=kLoop, calls=%fused_computation.87 | loop fusion | flops 92012544 | bytes 245366784 | tf_op jit(solution)/shard_map/concatenate | solution.py:87
  1023.7 29.8 %all-reduce = f32[384]{0:T(512)S(1)} all-reduce(f32[384]{0:T(512)S(1)} %dynamic-update-slice), channel_id=2, replica_groups=mesh['grp'=2,'fsdp'=16] {'fsdp'}, use_global_device_ids=true, to_apply=%add | all-reduce | flops 384 | bytes 3072
  1056.5 1059.0 %reduce-scatter.3.cloned.1.call-done = f32[96,19968]{1,0:T(8,128)} async-done(((f32[1536,19968]{1,0:T(8,128)}), f32[96,19968]{1,0:T(8,128)}) %reduce-scatter.3.cloned.1.call-update) | async-done | bytes 7667728 | tf_op jit(solution)/shard_map/reduce_scatter | solution.py:369
  2115.5 5.4 convert_element_type.137
  2121.6 10.0 fusion.90
  2131.5 14.2 fusion.113
  2145.7 3.0 fusion.105
  2151.7 2.5 multiply_reduce_fusion.1
  2155.7 2.6 fusion.109
  2158.2 83.1 %all-reduce.4.cloned.1.call-done = f32[1536,24]{0,1:T(8,128)} async-done(((f32[1536,24]{0,1:T(8,128)}), f32[1536,24]{0,1:T(8,128)}) %all-reduce.4.cloned.1.call-update) | async-done | bytes 147472 | tf_op jit(solution)/shard_map/psum | solution.py:376
  2242.9 54.2 %reduce-scatter.5.cloned.1.call-done = bf16[48,19968]{1,0:T(8,128)(2,1)} async-done(((bf16[96,19968]{1,0:T(8,128)(2,1)}), bf16[48,19968]{1,0:T(8,128)(2,1)}) %reduce-scatter.5.cloned.1.call-update) | async-done | bytes 1916944 | tf_op jit(solution)/shard_map/reduce_scatter | solution.py:372
  2297.1 3.1 fusion.87
  2300.2 40.2 %all-reduce.1 = (f32[]{:T(128)}, f32[4,1536]{1,0:T(4,128)S(1)}, f32[24]{0:T(128)S(1)}) all-reduce(f32[]{:T(128)} %fusion.87, f32[4,1536]{1,0:T(4,128)S(1)} %pad_maximum_fusion.7, f32[24]{0:T(128)S(1)} %copy-done.62), channel_id=1, replica_groups=mesh['grp'=2,'fsdp'=16] {'grp','fsdp'}, use_global_device_ids=true, to_apply=%region_32.33 | all-reduce | flops 6169 | bytes 49352 | tf_op jit(solution)/shard_map/psum | solution.py:376
  2347.3 9.0 multiply_subtract_fusion
  (369 shorter events, 137.7 us)
Async XLA Ops:
  7.2 5.2 copy-start.3
  7.2 132.0 %all-gather.10.cloned.1.call-start = ((), (), s32[]{:S(2)}) async-start(), calls=%async_computation.2 | async-start | bytes 19464192 | tf_op jit(solution)/shard_map/all_gather | solution.py:238
  11.7 218.4 %all-gather.12.cloned.1.call-start = ((), (), s32[]{:S(2)}) async-start(), calls=%async_computation.3 | async-start | bytes 6684672 | tf_op jit(solution)/shard_map/all_gather | solution.py:263
  12.4 152.1 %copy-start.48 = (f32[1536]{0:T(1024)}, f32[1536]{0:T(1024)S(1)}, u32[]{:S(2)}) copy-start(f32[1536]{0:T(1024)S(1)} %get-tuple-element.1191) | copy-start | bytes 18436
  12.4 161.9 %copy-start.36 = (f32[1536]{0:T(1024)}, f32[1536]{0:T(1024)S(1)}, u32[]{:S(2)}) copy-start(f32[1536]{0:T(1024)S(1)} %get-tuple-element.1192) | copy-start | bytes 18436
  147.1 494.2 %copy-start = (f32[128,6144]{1,0:T(8,128)}, f32[128,6144]{1,0:T(8,128)S(1)}, u32[]{:S(2)}) copy-start(f32[128,6144]{1,0:T(8,128)S(1)} %fusion.132) | copy-start | bytes 9437188
  167.0 126.2 %all-gather.14.cloned.1.call-start = ((), (), s32[]{:S(2)}) async-start(), calls=%async_computation.4 | async-start | bytes 6684672 | tf_op jit(solution)/shard_map/all_gather | solution.py:264
  167.9 190.9 %all-gather.16.cloned.1.call-start = ((), (), s32[]{:S(2)}) async-start(), calls=%async_computation.5 | async-start | bytes 4866048 | tf_op jit(solution)/shard_map/all_gather | solution.py:277
  169.5 346.0 %all-gather.18.cloned.1.call-start = ((), (), s32[]{:S(2)}) async-start(), calls=%async_computation.6 | async-start | bytes 25952256 | tf_op jit(solution)/shard_map/all_gather | solution.py:284
  171.7 440.7 %all-gather.20.cloned.1.call-start = ((), (), s32[]{:S(2)}) async-start(), calls=%async_computation.7 | async-start | bytes 12976128 | tf_op jit(solution)/shard_map/all_gather | solution.py:278
  173.5 501.8 %all-gather.22.cloned.1.call-start = ((), (), s32[]{:S(2)}) async-start(), calls=%async_computation.8 | async-start | bytes 6684672 | tf_op jit(solution)/shard_map/all_gather | solution.py:337
  174.3 610.6 %all-gather.24.cloned.1.call-start = ((), (), s32[]{:S(2)}) async-start(), calls=%async_computation.9 | async-start | bytes 6684672 | tf_op jit(solution)/shard_map/all_gather | solution.py:338
  328.2 6.0 copy-start.17
  328.2 6.0 copy-start.31
  345.5 17.4 copy-start.69
  358.7 5.1 copy-start.40
  363.4 275.5 %copy-start.60 = (f32[128]{0:T(128)}, f32[128]{0:T(128)S(1)}, u32[]{:S(2)}) copy-start(f32[128]{0:T(128)S(1)} %fusion.124) | copy-start | bytes 1540
  641.3 5.7 copy-start.24
  641.3 11.2 copy-start.56
  646.9 9.7 copy-start.12
  647.0 1468.5 %reduce-scatter.3.cloned.1.call-start = ((), (), s32[]{:S(2)}) async-start(), calls=%async_computation.10 | async-start | bytes 130351104 | tf_op jit(solution)/shard_map/reduce_scatter | solution.py:369
  691.7 14.2 copy-start.29
  691.7 36.7 %copy-start.25 = (bf16[128,1536]{1,0:T(8,128)(2,1)S(1)}, bf16[128,1536]{1,0:T(8,128)(2,1)}, u32[]{:S(2)}) copy-start(bf16[128,1536]{1,0:T(8,128)(2,1)} %copy-done.24) | copy-start | bytes 1179652
  691.7 36.9 %copy-start.23 = (bf16[128,1536]{1,0:T(8,128)(2,1)S(1)}, bf16[128,1536]{1,0:T(8,128)(2,1)}, u32[]{:S(2)}) copy-start(bf16[128,1536]{1,0:T(8,128)(2,1)} %get-tuple-element.1289) | copy-start | bytes 1179652
  691.7 57.6 %copy-start.13 = (bf16[128,1536]{1,0:T(8,128)(2,1)S(1)}, bf16[128,1536]{1,0:T(8,128)(2,1)}, u32[]{:S(2)}) copy-start(bf16[128,1536]{1,0:T(8,128)(2,1)} %multiply_convert_fusion.19) | copy-start | bytes 1179652
  731.0 23.2 copy-start.51
  749.3 5.0 copy-start.11
  754.2 10.2 copy-start.26
  801.2 15.2 copy-start.5
  801.2 15.2 copy-start.10
  801.2 15.2 copy-start.70
  816.4 99.8 %copy-start.6 = (f32[128,1536]{0,1:T(8,128)S(1)}, f32[128,1536]{0,1:T(8,128)}, u32[]{:S(2)}) copy-start(f32[128,1536]{0,1:T(8,128)} %copy.68) | copy-start | bytes 2359300
  842.4 5.8 copy-start.16
  854.4 4.9 copy-start.9
  854.4 4.9 copy-start.15
  863.2 5.8 copy-start.16
  875.2 4.9 copy-start.9
  883.9 5.8 copy-start.16
  904.7 5.8 copy-start.16
  913.0 12.2 copy-start.19
  916.2 24.9 %copy-start.20 = (bf16[128,1536]{1,0:T(8,128)(2,1)}, bf16[128,1536]{1,0:T(8,128)(2,1)S(1)}, u32[]{:S(2)}) copy-start(bf16[128,1536]{1,0:T(8,128)(2,1)S(1)} %copy.94) | copy-start | bytes 1179652
  923.9 17.2 copy-start.21
  925.3 15.9 copy-start.22
  1021.4 33.4 %copy-start.58 = (f32[128,24]{0,1:T(8,128)S(1)}, f32[128,24]{0,1:T(8,128)}, u32[]{:S(2)}) copy-start(f32[128,24]{0,1:T(8,128)} %get-tuple-element.1307) | copy-start | bytes 36868
  1021.4 34.1 %copy-start.4 = (bf16[1,128,1536]{2,1,0:T(8,128)(2,1)S(1)}, bf16[1,128,1536]{2,1,0:T(8,128)(2,1)}, u32[]{:S(2)}) copy-start(bf16[1,128,1536]{2,1,0:T(8,128)(2,1)} %param.26) | copy-start | bytes 1179652
  1021.4 34.1 %copy-start.37 = (f32[1536]{0:T(1024)S(1)}, f32[1536]{0:T(1024)}, u32[]{:S(2)}) copy-start(f32[1536]{0:T(1024)} %copy-done.36) | copy-start | bytes 18436
  1021.4 34.0 %copy-start.57 = (f32[128]{0:T(128)S(1)}, f32[128]{0:T(128)}, u32[]{:S(2)}) copy-start(f32[128]{0:T(128)} %fusion.123) | copy-start | bytes 1540
  1021.4 1219.9 %all-reduce.4.cloned.1.call-start = ((), (), s32[]{:S(2)}) async-start(), calls=%async_computation.12 | async-start | bytes 294912 | tf_op jit(solution)/shard_map/psum | solution.py:376
  1056.4 1064.5 %copy-start.59 = (f32[1536]{0:T(1024)S(1)}, f32[1536]{0:T(1024)}, u32[]{:S(2)}) copy-start(f32[1536]{0:T(1024)} %get-tuple-element.1185) | copy-start | bytes 18436
  1056.4 1065.1 %copy-start.2 = (f32[128,1536]{1,0:T(8,128)S(1)}, f32[128,1536]{1,0:T(8,128)}, u32[]{:S(2)}) copy-start(f32[128,1536]{1,0:T(8,128)} %copy-done.1) | copy-start | bytes 2359300
  1056.4 1240.6 %reduce-scatter.5.cloned.1.call-start = ((), (), s32[]{:S(2)}) async-start(), calls=%async_computation.11 | async-start | bytes 5750784 | tf_op jit(solution)/shard_map/reduce_scatter | solution.py:372
  2131.5 20.1 copy-start.8
  2145.7 10.0 copy-start.41
  2150.5 5.2 copy-start.14
  2150.5 195.1 %copy-start.30 = (f32[1536,24]{0,1:T(8,128)S(1)}, f32[1536,24]{0,1:T(8,128)}, u32[]{:S(2)}) copy-start(f32[1536,24]{0,1:T(8,128)} %param.34) | copy-start | bytes 442372
  2150.5 195.1 %copy-start.38 = (f32[1536,24]{0,1:T(8,128)S(1)}, f32[1536,24]{0,1:T(8,128)}, u32[]{:S(2)}) copy-start(f32[1536,24]{0,1:T(8,128)} %param.35) | copy-start | bytes 442372
  2151.7 148.6 %copy-start.62 = (f32[24]{0:T(128)S(1)}, f32[24]{0:T(128)}, u32[]{:S(2)}) copy-start(f32[24]{0:T(128)} %get-tuple-element.1286) | copy-start | bytes 292
  2151.7 192.7 %copy-start.65 = (f32[24]{0:T(128)S(1)}, f32[24]{0:T(128)}, u32[]{:S(2)}) copy-start(f32[24]{0:T(128)} %param.37) | copy-start | bytes 292
  2151.7 192.7 %copy-start.66 = (f32[24]{0:T(128)S(1)}, f32[24]{0:T(128)}, u32[]{:S(2)}) copy-start(f32[24]{0:T(128)} %param.38) | copy-start | bytes 292
  2151.7 192.7 %copy-start.67 = (f32[24]{0:T(128)S(1)}, f32[24]{0:T(128)}, u32[]{:S(2)}) copy-start(f32[24]{0:T(128)} %param.39) | copy-start | bytes 292
  2151.7 193.2 %copy-start.47 = (f32[4,1536]{1,0:T(4,128)S(1)}, f32[4,1536]{1,0:T(4,128)}, u32[]{:S(2)}) copy-start(f32[4,1536]{1,0:T(4,128)} %param.31) | copy-start | bytes 73732
  2151.7 193.2 %copy-start.54 = (f32[4,1536]{1,0:T(4,128)S(1)}, f32[4,1536]{1,0:T(4,128)}, u32[]{:S(2)}) copy-start(f32[4,1536]{1,0:T(4,128)} %param.32) | copy-start | bytes 73732
  2151.7 193.2 %copy-start.55 = (f32[4,1536]{1,0:T(4,128)S(1)}, f32[4,1536]{1,0:T(4,128)}, u32[]{:S(2)}) copy-start(f32[4,1536]{1,0:T(4,128)} %param.33) | copy-start | bytes 73732
  2151.7 193.8 %copy-start.39 = (f32[1536,24]{0,1:T(8,128)S(1)}, f32[1536,24]{0,1:T(8,128)}, u32[]{:S(2)}) copy-start(f32[1536,24]{0,1:T(8,128)} %param.36) | copy-start | bytes 442372
  (33 other events, 91.5 us)
Sparse Core Ops, SparseCore 0:
  11.8 127.3 all-gather.9
  167.1 62.9 all-gather.11
  232.4 60.7 all-gather.13
  296.5 62.1 all-gather.15
  362.0 153.4 all-gather.17
  518.2 94.0 all-gather.19
  615.2 60.0 all-gather.21
  677.7 63.0 all-gather.23
  1021.6 1093.8 reduce-scatter.2
  2121.5 119.8 all-reduce.3
  2244.2 52.8 reduce-scatter.4
where the time goes:
time: 2380 us; the launch traced here: 2360 us
  waiting for transfers between devices  1630 us (68%)
  matrix products  214 us (9%)
  local copies, waits for them, and re-layouts  194 us (8%)
  other arithmetic  146 us (6%)
  blocking collectives  137 us (6%)
    reduce_scatter x1, waiting for transfers between devices, shards(): lax.psum_scatter(grad_terms(pairs=attn_pairs + mlp_pairs), 'fsdp', scatte...  1060 us
    all_gather x1, waiting for transfers between devices, shards(): lax.all_gather(narrow[:, 5 * D:5 * D + 2 * F], ('grp', 'fsdp'), axis=0, t...  151 us
    all_gather x1, waiting for transfers between devices, shards(): lax.all_gather(narrow[:, :4 * D], ('grp', 'fsdp'), axis=0, tiled=True)  126 us
    all_gather x1, waiting for transfers between devices, shards(): lax.all_gather(narrow[:, 5 * D + 2 * F:], ('grp', 'fsdp'), axis=0, tiled=...  83.2 us
    psum x1, waiting for transfers between devices, shards(): lax.psum((jnp.sum(grad_weights * grad_weights), grad_gains, grad_forget,...  83.1 us
    concatenate x1, other arithmetic, grad_terms(): return jnp.concatenate(terms, axis=1)  80.2 us
    another operation x4, local copies, waits for them, and re-layouts, split_blocks(): return array.reshape((array.shape[0] // step, step) + array.shape[1:])  65.1 us
    reduce_scatter x1, waiting for transfers between devices, shards(): lax.psum_scatter(member_grads.astype(jnp.bfloat16), 'grp', scatter_dimens...  54.2 us
  transfers between devices with their start and end apart: 11, of which 10 were waited for; matrix products, arithmetic and copies ran while one was open for 12% of the time, Pallas kernels for 0%

commit v1 on v0

v1 whole, which is shorter than its diff:
```python
import functools

import jax
import jax.numpy as jnp
from jax import lax
from jax.experimental import pallas as pl
from jax.experimental.pallas import tpu as pltpu
from jax.sharding import PartitionSpec as P

D = 1536
H = 24
DH = 64
F = 4096
STEP = 5

EPS = 1e-06
BETA_ONE = 0.9
BETA_TWO = 0.95
ADAM_EPS = 1e-08
RATE_MATRIX = 0.1
RATE_GAIN = 1.2
RATE_BIAS = 3.0
DECAY = 0.1
CLIP = 1.0
NEGATIVE = -1e30

TP = 8
HEADS = H // TP
UNITS = F // TP
QKVG = HEADS * 4 * DH
WIDTH = QKVG + 3 * UNITS + 256
LANES = 128
ROWS = 256
BLOCK = 512
MESH = pl.DeviceIdType.MESH
HALF = jnp.bfloat16
FULL = jnp.float32
VMEM_BYTES = 56 * 1024 * 1024


def params(collective=None, **more):
    if collective is None:
        return pltpu.CompilerParams(vmem_limit_bytes=VMEM_BYTES, **more)
    return pltpu.CompilerParams(
        collective_id=collective, has_side_effects=True, vmem_limit_bytes=VMEM_BYTES, **more
    )


def flip(member, bits):
    for bit in (1, 2, 4):
        if bits & bit:
            member = member + bit - 2 * bit * lax.rem(lax.div(member, bit), 2)
    return member


def place():
    position = lax.axis_index("fsdp")
    return lax.axis_index("grp"), lax.div(position, TP), lax.rem(position, TP)


def greet(targets):
    barrier = pltpu.get_barrier_semaphore()
    for target in targets:
        pl.semaphore_signal(barrier, inc=1, device_id=target, device_id_type=MESH)
    pl.semaphore_wait(barrier, len(targets))


class Lines:
    def __init__(self, send, receive):
        self.send, self.receive, self.count, self.made = send, receive, 0, []

    def plan(self, source, target, device):
        copy = pltpu.make_async_remote_copy(
            src_ref=source,
            dst_ref=target,
            send_sem=self.send.at[self.count],
            recv_sem=self.receive.at[self.count],
            device_id=device,
            device_id_type=MESH,
        )
        self.count += 1
        self.made.append(copy)
        return copy


def dot(left, right, contract=(1, 0)):
    return lax.dot_general(
        left, right, (((contract[0],), (contract[1],)), ((), ())), preferred_element_type=FULL
    )


def rms_rows(value, gain):
    return value * lax.rsqrt(jnp.mean(value * value, axis=-1, keepdims=True) + EPS) * gain


def rms_back(value, gain, grad):
    inverse = lax.rsqrt(jnp.mean(value * value, axis=-1, keepdims=True) + EPS)
    normal = value * inverse
    scaled = grad * gain
    pulled = inverse * (scaled - normal * jnp.mean(scaled * normal, axis=-1, keepdims=True))
    return pulled, jnp.sum(grad * normal, axis=0, keepdims=True)


def start_counts(grps, groups):
    tokens = groups * TP - 1
    weights = (TP - 1) + (groups - 1) * TP + (grps - 1) * groups * TP
    return tokens + weights + (TP - 1)


def start_kernel(grps, groups, a_ref, c_ref, w_ref, span_ref, cot_ref, full_ref, send, receive, local):
    grp, group, member = place()

    def device(to_grp=0, to_group=0, bits=0):
        return (
            lax.rem(grp + to_grp, grps),
            lax.rem(group + to_group, groups) * TP + flip(member, bits),
        )

    greet(
        [device(bits=bits) for bits in range(1, TP)]
        + [device(to_group=step) for step in range(1, groups)]
        + [device(to_grp=step) for step in range(1, grps)]
    )
    lines = Lines(send, receive)
    tokens, cots, first, across, over = {}, {}, {}, {}, {}
    for back in range(groups):
        origin = lax.rem(group + back, groups)
        if back:
            tokens[back, 0] = lines.plan(a_ref, span_ref.at[group, member], device(to_group=groups - back))
        for bits in (1, 2, 4, 6):
            slot = span_ref.at[origin, member]
            source = a_ref if back == 0 else slot
            tokens[back, bits] = lines.plan(source, slot, device(bits=bits))
        for bits in (2, 4, 6):
            slot = span_ref.at[origin, flip(member, bits)]
            tokens[back, bits + 1] = lines.plan(slot, slot, device(bits=1))
    for bits in (1, 2, 4, 6):
        cots[bits] = lines.plan(c_ref, cot_ref.at[member], device(bits=bits))
    for bits in (2, 4, 6):
        slot = cot_ref.at[flip(member, bits)]
        cots[bits + 1] = lines.plan(slot, slot, device(bits=1))
    for bits in range(1, TP):
        first[bits] = lines.plan(w_ref.at[flip(member, bits)], full_ref.at[grp, group, member], device(bits=bits))
    for bits in range(TP):
        slot = full_ref.at[grp, group, flip(member, bits)]
        source = w_ref.at[member] if bits == 0 else slot
        for back in range(1, groups):
            across[back, bits] = lines.plan(source, slot, device(to_group=groups - back))
        for step in range(1, grps):
            over[step, 0, bits] = lines.plan(source, slot, device(to_grp=step))
        for back in range(1, groups):
            passed = full_ref.at[grp, lax.rem(group + back, groups), flip(member, bits)]
            for step in range(1, grps):
                over[step, back, bits] = lines.plan(passed, passed, device(to_grp=step))

    own = [
        pltpu.make_async_copy(a_ref, span_ref.at[group, member], local.at[0]),
        pltpu.make_async_copy(c_ref, cot_ref.at[member], local.at[1]),
        pltpu.make_async_copy(w_ref.at[member], full_ref.at[grp, group, member], local.at[2]),
    ]
    for back in range(1, groups):
        tokens[back, 0].start()
        across[back, 0].start()
    for bits in (2, 4, 6, 1):
        tokens[0, bits].start()
    for step in range(1, grps):
        over[step, 0, 0].start()
    for bits in range(1, TP):
        first[bits].start()
    for bits in (2, 4, 6, 1):
        cots[bits].start()
    for copy in own:
        copy.start()
    for bits in (2, 4, 6):
        tokens[0, bits].wait_recv()
        tokens[0, bits + 1].start()
    for bits in range(1, TP):
        first[bits].wait_recv()
        for back in range(1, groups):
            across[back, bits].start()
        for step in range(1, grps):
            over[step, 0, bits].start()
    for back in range(1, groups):
        tokens[back, 0].wait_recv()
        for bits in (2, 4, 6, 1):
            tokens[back, bits].start()
    for bits in (2, 4, 6):
        cots[bits].wait_recv()
        cots[bits + 1].start()
    for back in range(1, groups):
        for bits in (2, 4, 6):
            tokens[back, bits].wait_recv()
            tokens[back, bits + 1].start()
    for back in range(1, groups):
        for bits in range(TP):
            across[back, bits].wait_recv()
            for step in range(1, grps):
                over[step, back, bits].start()
    for back in range(groups):
        for bits in (1, 3, 5, 7):
            tokens[back, bits].wait_recv()
    for bits in (1, 3, 5, 7):
        cots[bits].wait_recv()
    for copy in over.values():
        copy.wait_recv()
    for copy in lines.made:
        copy.wait_send()
    for copy in own:
        copy.wait()


def start(low, cotangent, pack, grps, groups):
    rows, own = low.shape[0], pack.shape[1]
    count = start_counts(grps, groups)
    spec = pl.BlockSpec(memory_space=pl.ANY)
    return pl.pallas_call(
        functools.partial(start_kernel, grps, groups),
        out_shape=(
            jax.ShapeDtypeStruct((groups, TP, rows, D), HALF),
            jax.ShapeDtypeStruct((TP, rows, D), HALF),
            jax.ShapeDtypeStruct((grps, groups, TP, own, WIDTH), HALF),
        ),
        in_specs=[spec] * 3,
        out_specs=(spec,) * 3,
        scratch_shapes=[
            pltpu.SemaphoreType.DMA((count,)),
            pltpu.SemaphoreType.DMA((count,)),
            pltpu.SemaphoreType.DMA((3,)),
        ],
        compiler_params=params(1),
        name="start",
    )(low, cotangent, pack)


def column(value, lane):
    lanes = lax.broadcasted_iota(jnp.int32, value.shape, 1)
    return jnp.sum(jnp.where(lanes == lane, value, 0.0), axis=1, keepdims=True)


def three(value):
    high = value.astype(HALF).astype(FULL)
    rest = value - high
    middle = rest.astype(HALF).astype(FULL)
    return high, middle, (rest - middle).astype(HALF).astype(FULL)


def at_lanes(lanes, pairs, other):
    for lane, value in pairs:
        other = jnp.where(lanes == lane, value, other)
    return other


def halves_mean(value, lanes):
    lower = jnp.sum(jnp.where(lanes < DH, value, 0.0), axis=1, keepdims=True)
    upper = jnp.sum(jnp.where(lanes < DH, 0.0, value), axis=1, keepdims=True)
    return jnp.where(lanes < DH, lower, upper) * (1.0 / DH)


def project_kernel(a_ref, w_ref, f_ref, b_ref, g_ref, q_ref, k_ref, v_ref, p_ref, z_ref, s_ref, carry):
    @pl.when(pl.program_id(0) == 0)
    def clear():
        carry[...] = jnp.zeros_like(carry)

    low = a_ref[...]
    made = dot(low, w_ref[...])
    p_ref[...] = made
    logit = dot(low, f_ref[...]) + b_ref[...]
    z_ref[...] = logit
    log_gate = jnp.minimum(logit, 0.0) - jnp.log1p(jnp.exp(-jnp.abs(logit)))
    count = low.shape[0]
    row = lax.broadcasted_iota(jnp.int32, (count, count), 0)
    col = lax.broadcasted_iota(jnp.int32, (count, count), 1)
    sums = (
        lax.dot_general(
            jnp.where(col <= row, 1.0, 0.0),
            log_gate,
            (((1,), (0,)), ((), ())),
            precision=lax.Precision.HIGHEST,
            preferred_element_type=FULL,
        )
        + carry[0:1]
    )
    carry[0:1] = sums[count - 1 : count]
    s_ref[...] = sums
    lanes = lax.broadcasted_iota(jnp.int32, (count, LANES), 1)
    for head in range(HEADS):
        pair = made[:, 256 * head : 256 * head + LANES]
        value = made[:, 256 * head + LANES : 256 * head + 2 * LANES]
        normal = pair * lax.rsqrt(halves_mean(pair * pair, lanes) + EPS) * g_ref[head : head + 1]
        normal = normal.astype(HALF).astype(FULL)
        high, middle, least = three(column(sums, head))
        ones = jnp.where(lanes < DH + 6, 1.0, 0.0)
        q_ref[head] = jnp.where(
            lanes < DH,
            normal * (DH**-0.5),
            at_lanes(lanes, ((DH, high), (DH + 1, middle), (DH + 2, least)), ones),
        ).astype(HALF)
        ones = jnp.where(lanes < DH + 3, 1.0, 0.0)
        k_ref[head] = jnp.where(
            lanes < DH,
            pltpu.roll(normal, DH, 1),
            at_lanes(lanes, ((DH + 3, -high), (DH + 4, -middle), (DH + 5, -least)), ones),
        ).astype(HALF)
        v_ref[head] = jnp.where(lanes < DH, value, ones).astype(HALF)


def project(span, full, forget, bias, gains):
    tokens = span.shape[0]
    tile = pl.BlockSpec((HEADS, ROWS, LANES), lambda i: (0, i, 0))
    return pl.pallas_call(
        project_kernel,
        grid=(tokens // ROWS,),
        out_shape=(
            jax.ShapeDtypeStruct((HEADS, tokens, LANES), HALF),
            jax.ShapeDtypeStruct((HEADS, tokens, LANES), HALF),
            jax.ShapeDtypeStruct((HEADS, tokens, LANES), HALF),
            jax.ShapeDtypeStruct((tokens, QKVG), FULL),
            jax.ShapeDtypeStruct((tokens, LANES), FULL),
            jax.ShapeDtypeStruct((tokens, LANES), FULL),
        ),
        in_specs=[
            pl.BlockSpec((ROWS, D), lambda i: (i, 0)),
            pl.BlockSpec((D, QKVG), lambda i: (0, 0)),
            pl.BlockSpec((D, LANES), lambda i: (0, 0)),
            pl.BlockSpec((1, LANES), lambda i: (0, 0)),
            pl.BlockSpec((8, LANES), lambda i: (0, 0)),
        ],
        out_specs=(
            tile,
            tile,
            tile,
            pl.BlockSpec((ROWS, QKVG), lambda i: (i, 0)),
            pl.BlockSpec((ROWS, LANES), lambda i: (i, 0)),
            pl.BlockSpec((ROWS, LANES), lambda i: (i, 0)),
        ),
        scratch_shapes=[pltpu.VMEM((8, LANES), FULL)],
        compiler_params=params(),
        name="project",
    )(span, full, forget, bias, gains)


def sigmoid(value):
    return 1.0 / (1.0 + jnp.exp(-value))


def gates_of(made, lanes):
    second = [made[:, 256 * head + LANES : 256 * head + 2 * LANES] for head in range(HEADS)]
    left = jnp.where(lanes < DH, pltpu.roll(second[0], DH, 1), second[1])
    right = jnp.where(lanes < DH, pltpu.roll(second[2], DH, 1), 0.0)
    return left, right


def attend_kernel(where_ref, q_ref, k_ref, v_ref, p_ref, u_ref, o_ref, l_ref):
    count = q_ref.shape[1]
    before = where_ref[0] * (1024 // count) + pl.program_id(0)
    queries = [q_ref[head] for head in range(HEADS)]

    def visit(state, at, masked):
        new = []
        for head in range(HEADS):
            top, total, accum = state[head]
            scores = dot(queries[head], k_ref[head, pl.ds(at * count, count)], (1, 1))
            if masked:
                row = lax.broadcasted_iota(jnp.int32, scores.shape, 0)
                col = lax.broadcasted_iota(jnp.int32, scores.shape, 1)
                scores = jnp.where(col <= row, scores, NEGATIVE)
            high = jnp.maximum(top, jnp.max(scores, axis=1, keepdims=True))
            shrink = jnp.exp(top - high)
            weight = jnp.exp(scores - high)
            total = total * shrink + jnp.sum(weight, axis=1, keepdims=True)
            accum = accum * shrink + dot(weight.astype(HALF), v_ref[head, pl.ds(at * count, count)])
            new.append((high, total, accum))
        return tuple(new)

    state = tuple(
        (
            jnp.full((count, 1), NEGATIVE, FULL),
            jnp.zeros((count, 1), FULL),
            jnp.zeros((count, LANES), FULL),
        )
        for head in range(HEADS)
    )
    state = lax.fori_loop(0, before, lambda at, inner: visit(inner, at, False), state)
    state = visit(state, before, True)
    lanes = lax.broadcasted_iota(jnp.int32, (count, LANES), 1)
    out = [jnp.where(lanes < DH, accum / total, 0.0) for top, total, accum in state]
    left, right = gates_of(p_ref[...], lanes)
    pair = out[0] + pltpu.roll(out[1], DH, 1)
    o_ref[:, :LANES] = pair
    o_ref[:, LANES:] = out[2]
    u_ref[:, :LANES] = (pair * sigmoid(left)).astype(HALF)
    u_ref[:, LANES:] = (out[2] * sigmoid(right)).astype(HALF)
    logs = [top + jnp.log(total) for top, total, accum in state]
    l_ref[...] = at_lanes(lanes, tuple(enumerate(logs)), 0.0)


def attend(where, queries, keys, values, made, own):
    tokens = queries.shape[1]
    count = min(BLOCK, own)
    steps = own // count
    whole = pl.BlockSpec((HEADS, tokens, LANES), lambda i, w: (0, 0, 0))
    return pl.pallas_call(
        attend_kernel,
        grid_spec=pltpu.PrefetchScalarGridSpec(
            num_scalar_prefetch=1,
            grid=(steps,),
            in_specs=[
                pl.BlockSpec((HEADS, count, LANES), lambda i, w: (0, w[0] * steps + i, 0)),
                whole,
                whole,
                pl.BlockSpec((count, QKVG), lambda i, w: (w[0] * steps + i, 0)),
            ],
            out_specs=(
                pl.BlockSpec((count, 256), lambda i, w: (i, 0)),
                pl.BlockSpec((count, 256), lambda i, w: (i, 0)),
                pl.BlockSpec((count, LANES), lambda i, w: (i, 0)),
            ),
        ),
        out_shape=(
            jax.ShapeDtypeStruct((own, 256), HALF),
            jax.ShapeDtypeStruct((own, 256), FULL),
            jax.ShapeDtypeStruct((own, LANES), FULL),
        ),
        compiler_params=params(),
        name="attend",
    )(where, queries, keys, values, made)


def group_device(bits):
    grp, group, member = place()
    return (grp, group * TP + flip(member, bits))


def blocks_of(ref, core):
    value = ref[:, pl.ds(core, 1)]
    return value.reshape(ref.shape[0] * ref.shape[2], ref.shape[3])


def sum_plan(lines, stage):
    give, take, out, came = stage
    sibling = [lines.plan(give.at[at], take.at[at], group_device(1)) for at in range(4)]
    others = [lines.plan(out.at[at], came.at[at], group_device(bits)) for at, bits in enumerate((2, 4, 6))]
    return sibling, others


def sum_send(pairs, stage, plan, mine):
    give, take, out, came = stage
    sibling, others = plan
    grp, group, member = place()
    core, chip = lax.rem(member, 2), lax.div(member, 2)
    count = give.shape[1]
    theirs = sum(dot(blocks_of(left, 1 - core), right[...], (1, 1)) for left, right in pairs)
    mine[...] = theirs.reshape(4, count, D)
    order = [lax.div(flip(member, bits), 2) for bits in (2, 4, 6, 0)]
    for at in range(4):
        give[at] = mine[order[at]].astype(HALF)
        sibling[at].start()
    own = sum(dot(blocks_of(left, core), right[...], (1, 1)) for left, right in pairs)
    mine[...] = own.reshape(4, count, D)
    for at in range(3):
        sibling[at].wait_recv()
        out[at] = (mine[order[at]] + take[at].astype(FULL)).astype(HALF)
        others[at].start()
    sibling[3].wait_recv()
    return mine[chip] + take[3].astype(FULL)


def sum_take(total, stage, plan):
    give, take, out, came = stage
    for at in range(3):
        plan[1][at].wait_recv()
        total = total + came[at].astype(FULL)
    return total


def sum_scratch(rows):
    return [
        pltpu.VMEM((4, rows, D), HALF),
        pltpu.VMEM((4, rows, D), HALF),
        pltpu.VMEM((3, rows, D), HALF),
        pltpu.VMEM((3, rows, D), HALF),
    ]


def gather_plan(lines, block, all_ref):
    grp, group, member = place()
    plan = {bits: lines.plan(block, all_ref.at[member], group_device(bits)) for bits in (2, 4, 6, 1)}
    for bits in (2, 4, 6):
        slot = all_ref.at[flip(member, bits)]
        plan[bits + 1] = lines.plan(slot, slot, group_device(1))
    return plan


def gather_run(plan, own):
    own.start()
    for bits in (2, 4, 6, 1):
        plan[bits].start()
    for bits in (2, 4, 6):
        plan[bits].wait_recv()
        plan[bits + 1].start()
    for bits in (1, 3, 5, 7):
        plan[bits].wait_recv()
    own.wait()


def mix_kernel(u_ref, w_ref, x_ref, g_ref, y_ref, all_ref, mine, block, give, take, out, came, send, receive, local):
    greet([group_device(bits) for bits in (1, 2, 4, 6)])
    member = place()[2]
    lines = Lines(send, receive)
    stage = (give, take, out, came)
    sums = sum_plan(lines, stage)
    gathered = gather_plan(lines, block, all_ref)
    total = sum_take(sum_send([(u_ref, w_ref)], stage, sums, mine), stage, sums)
    mixed = x_ref[...].astype(FULL) + total
    y_ref[...] = mixed
    block[...] = rms_rows(mixed, g_ref[...]).astype(HALF)
    gather_run(gathered, pltpu.make_async_copy(block, all_ref.at[member], local.at[0]))
    for copy in lines.made:
        copy.wait_send()


def whole_spec(shape):
    zeros = (0,) * len(shape)
    return pl.BlockSpec(shape, lambda i: zeros)


def weight_spec(columns, at):
    return pl.BlockSpec((D, columns), lambda i: (0, at))


def mix(gated, full, source, gain):
    rows = source.shape[0]
    return pl.pallas_call(
        mix_kernel,
        grid=(1,),
        out_shape=(
            jax.ShapeDtypeStruct((rows, D), FULL),
            jax.ShapeDtypeStruct((TP, rows, D), HALF),
        ),
        in_specs=[
            whole_spec((4, 2, rows, 256)),
            weight_spec(256, (QKVG + 3 * UNITS) // 256),
            whole_spec((rows, D)),
            whole_spec((1, D)),
        ],
        out_specs=(whole_spec((rows, D)), pl.BlockSpec(memory_space=pl.ANY)),
        scratch_shapes=[pltpu.VMEM((4, rows, D), FULL), pltpu.VMEM((rows, D), HALF)]
        + sum_scratch(rows)
        + [
            pltpu.SemaphoreType.DMA((14,)),
            pltpu.SemaphoreType.DMA((14,)),
            pltpu.SemaphoreType.DMA((1,)),
        ],
        compiler_params=params(2),
        name="mix",
    )(gated.reshape(4, 2, rows, 256), full, source, gain)


def unmix_kernel(
    d_ref, wgu_ref, m_ref, wd_ref, x_ref, g_ref, c_ref,
    y_ref, dx_ref, dg_ref, all_ref,
    mine, block, give, take, out, came, give2, take2, out2, came2, send, receive, local,
):
    greet([group_device(bits) for bits in (1, 2, 4, 6)])
    member = place()[2]
    lines = Lines(send, receive)
    stage = (give, take, out, came)
    stage2 = (give2, take2, out2, came2)
    sums = sum_plan(lines, stage)
    sums2 = sum_plan(lines, stage2)
    gathered = gather_plan(lines, block, all_ref)
    total = sum_send([(d_ref, wgu_ref)], stage, sums, mine)
    forward = sum_send([(m_ref, wd_ref)], stage2, sums2, mine)
    total = sum_take(total, stage, sums)
    mixed = x_ref[...]
    pulled, dgain = rms_back(mixed, g_ref[...], total)
    grad = c_ref[...].astype(FULL) + pulled
    dx_ref[...] = grad
    dg_ref[...] = dgain
    block[...] = grad.astype(HALF)
    gather_run(gathered, pltpu.make_async_copy(block, all_ref.at[member], local.at[0]))
    y_ref[...] = (mixed + sum_take(forward, stage2, sums2)).astype(HALF)
    for copy in lines.made:
        copy.wait_send()


def unmix(grads, hidden, full, mixed, gain, returned):
    rows = mixed.shape[0]
    return pl.pallas_call(
        unmix_kernel,
        grid=(1,),
        out_shape=(
            jax.ShapeDtypeStruct((rows, D), HALF),
            jax.ShapeDtypeStruct((rows, D), FULL),
            jax.ShapeDtypeStruct((1, D), FULL),
            jax.ShapeDtypeStruct((TP, rows, D), HALF),
        ),
        in_specs=[
            whole_spec((4, 2, rows, 2 * UNITS)),
            pl.BlockSpec((D, 2 * UNITS), lambda i: (0, 0)),
            whole_spec((4, 2, rows, UNITS)),
            pl.BlockSpec((D, UNITS), lambda i: (0, 0)),
            whole_spec((rows, D)),
            whole_spec((1, D)),
            whole_spec((rows, D)),
        ],
        out_specs=(
            whole_spec((rows, D)),
            whole_spec((rows, D)),
            whole_spec((1, D)),
            pl.BlockSpec(memory_space=pl.ANY),
        ),
        scratch_shapes=[pltpu.VMEM((4, rows, D), FULL), pltpu.VMEM((rows, D), HALF)]
        + sum_scratch(rows) * 2
        + [
            pltpu.SemaphoreType.DMA((21,)),
            pltpu.SemaphoreType.DMA((21,)),
            pltpu.SemaphoreType.DMA((1,)),
        ],
        compiler_params=params(3),
        name="unmix",
    )(
        grads.reshape(4, 2, rows, 2 * UNITS),
        full[:, QKVG : QKVG + 2 * UNITS],
        hidden.reshape(4, 2, rows, UNITS),
        full[:, QKVG + 2 * UNITS : QKVG + 3 * UNITS],
        mixed,
        gain,
        returned,
    )


def finish_kernel(
    p_ref, w_ref, z_ref, f_ref, x_ref, g_ref, d_ref, y_ref, dg_ref, mine, give, take, out, came, send, receive
):
    greet([group_device(bits) for bits in (1, 2, 4, 6)])
    lines = Lines(send, receive)
    stage = (give, take, out, came)
    sums = sum_plan(lines, stage)
    total = sum_send([(p_ref, w_ref), (z_ref, f_ref)], stage, sums, mine)
    total = sum_take(total, stage, sums)
    pulled, dgain = rms_back(x_ref[...].astype(FULL), g_ref[...], total)
    y_ref[...] = (d_ref[...] + pulled).astype(HALF)
    dg_ref[...] = dgain
    for copy in lines.made:
        copy.wait_send()


def finish(projected, full, logits, forget, source, gain, grad):
    rows = source.shape[0]
    return pl.pallas_call(
        finish_kernel,
        grid=(1,),
        out_shape=(
            jax.ShapeDtypeStruct((rows, D), HALF),
            jax.ShapeDtypeStruct((1, D), FULL),
        ),
        in_specs=[
            whole_spec((4, 2, rows, QKVG)),
            weight_spec(QKVG, 0),
            whole_spec((4, 2, rows, LANES)),
            whole_spec((D, LANES)),
            whole_spec((rows, D)),
            whole_spec((1, D)),
            whole_spec((rows, D)),
        ],
        out_specs=(whole_spec((rows, D)), whole_spec((1, D))),
        scratch_shapes=[pltpu.VMEM((4, rows, D), FULL)]
        + sum_scratch(rows)
        + [pltpu.SemaphoreType.DMA((7,)), pltpu.SemaphoreType.DMA((7,))],
        compiler_params=params(4),
        name="finish",
    )(
        projected.reshape(4, 2, rows, QKVG),
        full,
        logits.reshape(4, 2, rows, LANES),
        forget,
        source,
        gain,
        grad,
    )


def feed_kernel(a_ref, c_ref, wgu_ref, wd_ref, m_ref, d_ref):
    made = dot(a_ref[...], wgu_ref[...])
    gate, up = made[:, :UNITS], made[:, UNITS:]
    sig = sigmoid(gate)
    swish = gate * sig
    m_ref[...] = (swish * up).astype(HALF)
    grad = dot(c_ref[...], wd_ref[...])
    d_ref[:, :UNITS] = (grad * up * sig * (1.0 + gate * (1.0 - sig))).astype(HALF)
    d_ref[:, UNITS:] = (grad * swish).astype(HALF)


def feed(second, returned, full):
    tokens = second.shape[0]
    return pl.pallas_call(
        feed_kernel,
        grid=(tokens // ROWS,),
        out_shape=(
            jax.ShapeDtypeStruct((tokens, UNITS), HALF),
            jax.ShapeDtypeStruct((tokens, 2 * UNITS), HALF),
        ),
        in_specs=[
            pl.BlockSpec((ROWS, D), lambda i: (i, 0)),
            pl.BlockSpec((ROWS, D), lambda i: (i, 0)),
            pl.BlockSpec((D, 2 * UNITS), lambda i: (0, 0)),
            pl.BlockSpec((D, UNITS), lambda i: (0, 0)),
        ],
        out_specs=(
            pl.BlockSpec((ROWS, UNITS), lambda i: (i, 0)),
            pl.BlockSpec((ROWS, 2 * UNITS), lambda i: (i, 0)),
        ),
        compiler_params=params(),
        name="feed",
    )(second, returned, full[:, QKVG : QKVG + 2 * UNITS], full[:, QKVG + 2 * UNITS : QKVG + 3 * UNITS])


def ungate_kernel(where_ref, d_ref, w_ref, o_ref, p_ref, l_ref, s_ref, q_ref, do_ref, qb_ref, dg_ref, pack_ref):
    grad = dot(d_ref[...], w_ref[...])
    count = grad.shape[0]
    lanes = lax.broadcasted_iota(jnp.int32, (count, LANES), 1)
    gates = gates_of(p_ref[...], lanes)
    heads = []
    sent = []
    for at in range(2):
        part = grad[:, LANES * at : LANES * (at + 1)]
        attended = o_ref[:, LANES * at : LANES * (at + 1)]
        sig = sigmoid(gates[at])
        low = (part * sig).astype(HALF).astype(FULL)
        sent.append(low)
        dg_ref[:, LANES * at : LANES * (at + 1)] = part * attended * sig * (1.0 - sig)
        product = low * attended
        heads.append((low, jnp.sum(jnp.where(lanes < DH, product, 0.0), axis=1, keepdims=True)))
        if at == 0:
            heads.append(
                (
                    pltpu.roll(low, DH, 1),
                    jnp.sum(jnp.where(lanes < DH, 0.0, product), axis=1, keepdims=True),
                )
            )
    extra = jnp.zeros_like(lanes, FULL)
    for head, (low, delta) in enumerate(heads):
        minus = three(-delta)
        decay = three(column(s_ref[...], head) - column(l_ref[...], head))
        do_ref[head] = jnp.where(
            lanes < DH, low, at_lanes(lanes, [(DH + i, minus[i]) for i in range(3)], 0.0)
        ).astype(HALF)
        qb_ref[head] = at_lanes(
            lanes, [(DH + i, decay[i]) for i in range(3)], q_ref[head].astype(FULL)
        ).astype(HALF)
        extra = at_lanes(
            lanes,
            [(DH + 6 * head + i, minus[i]) for i in range(3)] + [(DH + 6 * head + 3 + i, decay[i]) for i in range(3)],
            extra,
        )
    pack_ref[:, :LANES] = sent[0].astype(HALF)
    pack_ref[:, LANES:] = jnp.where(lanes < DH, sent[1], extra).astype(HALF)


def ungate(where, grads, full, attended, made, logs, sums, queries):
    own = grads.shape[0]
    steps = own // ROWS
    head_tile = pl.BlockSpec((HEADS, ROWS, LANES), lambda i, w: (0, i, 0))
    return pl.pallas_call(
        ungate_kernel,
        grid_spec=pltpu.PrefetchScalarGridSpec(
            num_scalar_prefetch=1,
            grid=(steps,),
            in_specs=[
                pl.BlockSpec((ROWS, D), lambda i, w: (i, 0)),
                pl.BlockSpec((D, 256), lambda i, w: (0, (QKVG + 3 * UNITS) // 256)),
                pl.BlockSpec((ROWS, 256), lambda i, w: (i, 0)),
                pl.BlockSpec((ROWS, QKVG), lambda i, w: (w[0] * steps + i, 0)),
                pl.BlockSpec((ROWS, LANES), lambda i, w: (i, 0)),
                pl.BlockSpec((ROWS, LANES), lambda i, w: (w[0] * steps + i, 0)),
                pl.BlockSpec((HEADS, ROWS, LANES), lambda i, w: (0, w[0] * steps + i, 0)),
            ],
            out_specs=(
                head_tile,
                head_tile,
                pl.BlockSpec((ROWS, 256), lambda i, w: (i, 0)),
                pl.BlockSpec((ROWS, 256), lambda i, w: (i, 0)),
            ),
        ),
        out_shape=(
            jax.ShapeDtypeStruct((HEADS, own, LANES), HALF),
            jax.ShapeDtypeStruct((HEADS, own, LANES), HALF),
            jax.ShapeDtypeStruct((own, 256), FULL),
            jax.ShapeDtypeStruct((own, 256), HALF),
        ),
        compiler_params=params(),
        name="ungate",
    )(where, grads, full, attended, made, logs, sums, queries)


def pieces(scores, product, masked, transposed):
    prob = jnp.exp(scores)
    if masked:
        row = lax.broadcasted_iota(jnp.int32, scores.shape, 0)
        col = lax.broadcasted_iota(jnp.int32, scores.shape, 1)
        keep = row <= col if transposed else col <= row
        prob = jnp.where(keep, prob, 0.0)
    return prob.astype(HALF), (prob * product).astype(HALF)


def own_kernel(where_ref, q_ref, do_ref, k_ref, v_ref, dq_ref, dk_ref, dv_ref):
    count = min(BLOCK, q_ref.shape[1])
    steps = q_ref.shape[1] // count
    before = where_ref[0] * steps
    dk_ref[0] = jnp.zeros_like(dk_ref[0])
    dv_ref[0] = jnp.zeros_like(dv_ref[0])
    for at in range(steps):
        here = pl.ds(at * count, count)
        query, grad = q_ref[0, here], do_ref[0, here]

        def earlier(step, total):
            there = pl.ds(step * count, count)
            key = k_ref[0, there]
            prob, dscore = pieces(
                dot(query, key, (1, 1)), dot(grad, v_ref[0, there], (1, 1)), False, False
            )
            return total + dot(dscore, key)

        total = lax.fori_loop(0, before, earlier, jnp.zeros((count, LANES), FULL))
        for step in range(at + 1):
            there = pl.ds((before + step) * count, count)
            key = k_ref[0, there]
            prob, dscore = pieces(
                dot(key, query, (1, 1)), dot(v_ref[0, there], grad, (1, 1)), step == at, True
            )
            local = pl.ds(step * count, count)
            dk_ref[0, local] += dot(dscore, query)
            dv_ref[0, local] += dot(prob, grad)
            total = total + dot(dscore, key, (0, 0))
        dq_ref[0, here] = total


def own_back(where, queries, grads, keys, values):
    own, tokens = queries.shape[1], keys.shape[1]
    mine = pl.BlockSpec((1, own, LANES), lambda h, w: (h, 0, 0))
    whole = pl.BlockSpec((1, tokens, LANES), lambda h, w: (h, 0, 0))
    return pl.pallas_call(
        own_kernel,
        grid_spec=pltpu.PrefetchScalarGridSpec(
            num_scalar_prefetch=1,
            grid=(HEADS,),
            in_specs=[mine, mine, whole, whole],
            out_specs=(mine, mine, mine),
        ),
        out_shape=(jax.ShapeDtypeStruct((HEADS, own, LANES), FULL),) * 3,
        compiler_params=params(),
        name="own_back",
    )(where, queries, grads, keys, values)


def later_kernel(where_ref, q_ref, pack_ref, k_ref, v_ref, dk_in, dv_in, dk_ref, dv_ref, late_ref):
    own = k_ref.shape[1]
    head = pl.program_id(0)
    count = min(BLOCK, own)
    steps = own // count
    group, groups = where_ref[0], where_ref[1]
    dk_ref[0] = jnp.zeros_like(dk_ref[0])
    dv_ref[0] = dv_in[0]
    lanes = lax.broadcasted_iota(jnp.int32, (count, LANES), 1)

    def visit(at, carry):
        sent = pack_ref[pl.ds(at * count, count)].astype(FULL)
        left, right = sent[:, :LANES], sent[:, LANES:]
        grad = jnp.where(head == 0, left, jnp.where(head == 1, pltpu.roll(left, DH, 1), right))
        minus = [column(right, DH + 6 * head + i) for i in range(3)]
        decay = [column(right, DH + 6 * head + 3 + i) for i in range(3)]
        grad = jnp.where(
            lanes < DH, grad, at_lanes(lanes, [(DH + i, minus[i]) for i in range(3)], 0.0)
        ).astype(HALF)
        query = q_ref[0, pl.ds((group + 1) * own + at * count, count)].astype(FULL)
        query = at_lanes(lanes, [(DH + i, decay[i]) for i in range(3)], query).astype(HALF)
        for step in range(steps):
            here = pl.ds(step * count, count)
            prob, dscore = pieces(
                dot(k_ref[0, here], query, (1, 1)), dot(v_ref[0, here], grad, (1, 1)), False, True
            )
            dk_ref[0, here] += dot(dscore, query)
            dv_ref[0, here] += dot(prob, grad)
        return carry

    lax.fori_loop(0, (groups - 1 - group) * steps, visit, 0)
    late_ref[0] = jnp.broadcast_to(jnp.sum(dk_ref[0], axis=0, keepdims=True), (8, LANES))
    dk_ref[0] += dk_in[0]


def later_back(where, queries, pack, keys, values, dkeys, dvalues):
    own, tokens = dkeys.shape[1], keys.shape[1]
    mine = pl.BlockSpec((1, own, LANES), lambda h, w: (h, 0, 0))
    here = pl.BlockSpec((1, own, LANES), lambda h, w: (h, w[0], 0))
    return pl.pallas_call(
        later_kernel,
        grid_spec=pltpu.PrefetchScalarGridSpec(
            num_scalar_prefetch=1,
            grid=(HEADS,),
            in_specs=[
                pl.BlockSpec((1, tokens, LANES), lambda h, w: (h, 0, 0)),
                pl.BlockSpec(pack.shape, lambda h, w: (0, 0)),
                here,
                here,
                mine,
                mine,
            ],
            out_specs=(mine, mine, pl.BlockSpec((1, 8, LANES), lambda h, w: (h, 0, 0))),
        ),
        out_shape=(
            jax.ShapeDtypeStruct((HEADS, own, LANES), FULL),
            jax.ShapeDtypeStruct((HEADS, own, LANES), FULL),
            jax.ShapeDtypeStruct((HEADS, 8, LANES), FULL),
        ),
        compiler_params=params(),
        name="later_back",
    )(where, queries, pack, keys, values, dkeys, dvalues)


def unproject_kernel(
    where_ref, dq_ref, dk_ref, dv_ref, dg_ref, p_ref, z_ref, g_ref, late_ref, dp_ref, dz_ref, gain_ref, bias_ref, carry
):
    @pl.when(pl.program_id(0) == 0)
    def clear():
        carry[0:1] = late_ref[...]
        gain_ref[...] = jnp.zeros_like(gain_ref)
        bias_ref[...] = jnp.zeros_like(bias_ref)

    count = p_ref.shape[0]
    lanes = lax.broadcasted_iota(jnp.int32, (count, LANES), 1)
    sums = jnp.zeros((count, LANES), FULL)
    gates = [
        pltpu.roll(dg_ref[:, :LANES], DH, 1),
        dg_ref[:, :LANES],
        pltpu.roll(dg_ref[:, LANES:], DH, 1),
    ]
    for head in range(HEADS):
        dquery, dkey = dq_ref[head], dk_ref[head]
        sums = jnp.where(lanes == head, column(dquery, DH) - column(dkey, DH + 3), sums)
        grad = jnp.where(lanes < DH, dquery * (DH**-0.5), pltpu.roll(dkey, DH, 1))
        pair = p_ref[:, 256 * head : 256 * head + LANES]
        inverse = lax.rsqrt(halves_mean(pair * pair, lanes) + EPS)
        normal = pair * inverse
        scaled = grad * g_ref[head : head + 1]
        gain_ref[head : head + 1] += jnp.sum(grad * normal, axis=0, keepdims=True)
        pulled = inverse * (scaled - normal * halves_mean(scaled * normal, lanes))
        dp_ref[:, 256 * head : 256 * head + LANES] = pulled.astype(HALF)
        dp_ref[:, 256 * head + LANES : 256 * head + 2 * LANES] = jnp.where(
            lanes < DH, dv_ref[head], gates[head]
        ).astype(HALF)
    row = lax.broadcasted_iota(jnp.int32, (count, count), 0)
    col = lax.broadcasted_iota(jnp.int32, (count, count), 1)
    later = (
        lax.dot_general(
            jnp.where(col >= row, 1.0, 0.0),
            sums,
            (((1,), (0,)), ((), ())),
            precision=lax.Precision.HIGHEST,
            preferred_element_type=FULL,
        )
        + carry[0:1]
    )
    carry[0:1] = later[0:1]
    low = jnp.where(lanes < HEADS, later * sigmoid(-z_ref[...]), 0.0).astype(HALF)
    dz_ref[...] = low
    bias_ref[0:1] += jnp.sum(low.astype(FULL), axis=0, keepdims=True)


def unproject(where, dqueries, dkeys, dvalues, dgates, made, logits, gains, late):
    own = dqueries.shape[1]
    steps = own // ROWS
    head_tile = pl.BlockSpec((HEADS, ROWS, LANES), lambda i, w: (0, steps - 1 - i, 0))
    small = pl.BlockSpec((8, LANES), lambda i, w: (0, 0))
    return pl.pallas_call(
        unproject_kernel,
        grid_spec=pltpu.PrefetchScalarGridSpec(
            num_scalar_prefetch=1,
            grid=(steps,),
            in_specs=[
                head_tile,
                head_tile,
                head_tile,
                pl.BlockSpec((ROWS, 256), lambda i, w: (steps - 1 - i, 0)),
                pl.BlockSpec((ROWS, QKVG), lambda i, w: (w[0] * steps + steps - 1 - i, 0)),
                pl.BlockSpec((ROWS, LANES), lambda i, w: (w[0] * steps + steps - 1 - i, 0)),
                small,
                pl.BlockSpec((1, LANES), lambda i, w: (0, 0)),
            ],
            out_specs=(
                pl.BlockSpec((ROWS, QKVG), lambda i, w: (steps - 1 - i, 0)),
                pl.BlockSpec((ROWS, LANES), lambda i, w: (steps - 1 - i, 0)),
                small,
                small,
            ),
            scratch_shapes=[pltpu.VMEM((8, LANES), FULL)],
        ),
        out_shape=(
            jax.ShapeDtypeStruct((own, QKVG), HALF),
            jax.ShapeDtypeStruct((own, LANES), HALF),
            jax.ShapeDtypeStruct((8, LANES), FULL),
            jax.ShapeDtypeStruct((8, LANES), FULL),
        ),
        compiler_params=params(),
        name="unproject",
    )(where, dqueries, dkeys, dvalues, dgates, made, logits, gains, late)


def return_counts(grps, groups):
    return (grps - 1) * groups * TP + (groups - 1) * TP + TP - 1


def return_kernel(grps, groups, g_ref, o_ref, mine, over_got, across_out, across_got, last, send, receive, local):
    grp, group, member = place()

    def device(to_grp=0, to_group=0, bits=0):
        return (
            lax.rem(grp + to_grp, grps),
            lax.rem(group + to_group, groups) * TP + flip(member, bits),
        )

    greet(
        [device(bits=bits) for bits in range(1, TP)]
        + [device(to_group=step) for step in range(1, groups)]
        + [device(to_grp=step) for step in range(1, grps)]
    )
    lines = Lines(send, receive)
    over, across, home = {}, {}, {}
    for ahead in list(range(1, groups)) + [0]:
        there = lax.rem(group + ahead, groups)
        for bits in range(TP):
            for step in range(1, grps):
                over[step, ahead, bits] = lines.plan(
                    g_ref.at[lax.rem(grp + step, grps), there, flip(member, bits)],
                    over_got.at[step - 1, ahead, bits],
                    device(to_grp=step),
                )
            if ahead:
                across[ahead, bits] = lines.plan(
                    across_out.at[ahead - 1, bits], across_got.at[ahead - 1, bits], device(to_group=ahead)
                )
            elif bits:
                home[bits] = lines.plan(last.at[bits], o_ref.at[member], device(bits=bits))
    own = pltpu.make_async_copy(g_ref.at[grp], mine, local.at[0])
    own.start()
    for copy in over.values():
        copy.start()
    own.wait()
    for ahead in range(1, groups):
        there = lax.rem(group + ahead, groups)
        for bits in range(TP):
            total = mine[there, flip(member, bits)].astype(FULL)
            for step in range(1, grps):
                over[step, ahead, bits].wait_recv()
                total = total + over_got[step - 1, ahead, bits].astype(FULL)
            across_out[ahead - 1, bits] = total.astype(HALF)
            across[ahead, bits].start()
    for bits in list(range(1, TP)) + [0]:
        total = mine[group, flip(member, bits)].astype(FULL)
        for step in range(1, grps):
            over[step, 0, bits].wait_recv()
            total = total + over_got[step - 1, 0, bits].astype(FULL)
        for ahead in range(1, groups):
            across[ahead, bits].wait_recv()
            total = total + across_got[ahead - 1, bits].astype(FULL)
        last[bits] = total.astype(HALF)
        if bits:
            home[bits].start()
    keep = pltpu.make_async_copy(last.at[0], o_ref.at[member], local.at[0])
    keep.start()
    for copy in home.values():
        copy.wait_recv()
    keep.wait()
    for copy in lines.made:
        copy.wait_send()


def give_back(grads, grps, groups):
    own, width = grads.shape[3], grads.shape[4]
    count = return_counts(grps, groups)
    spec = pl.BlockSpec(memory_space=pl.ANY)
    return pl.pallas_call(
        functools.partial(return_kernel, grps, groups),
        out_shape=jax.ShapeDtypeStruct((TP, own, width), HALF),
        in_specs=[spec],
        out_specs=spec,
        scratch_shapes=[
            pltpu.VMEM((groups, TP, own, width), HALF),
            pltpu.VMEM((grps - 1, groups, TP, own, width), HALF),
            pltpu.VMEM((groups - 1, TP, own, width), HALF),
            pltpu.VMEM((groups - 1, TP, own, width), HALF),
            pltpu.VMEM((TP, own, width), HALF),
            pltpu.SemaphoreType.DMA((count,)),
            pltpu.SemaphoreType.DMA((count,)),
            pltpu.SemaphoreType.DMA((1,)),
        ],
        compiler_params=params(5),
        name="give_back",
    )(grads)


def total_kernel(bits, value_ref, out_ref, total, got, send, receive):
    grp, position = lax.axis_index("grp"), lax.axis_index("fsdp")

    def partner(bit):
        if bit == 0:
            return (1 - grp, position)
        return (grp, position + bit - 2 * bit * lax.rem(lax.div(position, bit), 2))

    greet([partner(bit) for bit in bits])
    lines = Lines(send, receive)
    out_ref[...] = value_ref[...]
    for at, bit in enumerate(bits):
        total[at] = out_ref[...]
        copy = lines.plan(total.at[at], got.at[at], partner(bit))
        copy.start()
        copy.wait_recv()
        out_ref[...] += got[at]
    for copy in lines.made:
        copy.wait_send()


def total_of(value, collective):
    bits, bit = [], 1
    while bit < lax.axis_size("fsdp"):
        bits.append(bit)
        bit *= 2
    if lax.axis_size("grp") == 2:
        bits.append(0)
    spec = pl.BlockSpec(memory_space=pltpu.VMEM)
    return pl.pallas_call(
        functools.partial(total_kernel, tuple(bits)),
        out_shape=jax.ShapeDtypeStruct(value.shape, FULL),
        in_specs=[spec],
        out_specs=spec,
        scratch_shapes=[
            pltpu.VMEM((len(bits),) + value.shape, FULL),
            pltpu.VMEM((len(bits),) + value.shape, FULL),
            pltpu.SemaphoreType.DMA((len(bits),)),
            pltpu.SemaphoreType.DMA((len(bits),)),
        ],
        compiler_params=params(collective),
        name="total_of",
    )(value)


def adam(value, first, second, grad, rate, decay):
    first = BETA_ONE * first + (1.0 - BETA_ONE) * grad
    second = BETA_TWO * second + (1.0 - BETA_TWO) * grad * grad
    unbiased_first = first / (1.0 - BETA_ONE**STEP)
    unbiased_second = second / (1.0 - BETA_TWO**STEP)
    value = value - rate * (unbiased_first / (jnp.sqrt(unbiased_second) + ADAM_EPS) + decay * value)
    return (value, first, second)


def pack_columns(weights):
    rows = weights.shape[0]
    low = weights.astype(HALF)
    edge = 5 * D + 2 * F
    heads = low[:, : 4 * D].reshape(rows, 4, TP, HEADS, DH).transpose(2, 0, 3, 1, 4).reshape(TP, rows, QKVG)
    out = low[:, 4 * D : 5 * D].reshape(rows, TP, HEADS * DH).transpose(1, 0, 2)
    both = low[:, 5 * D : edge].reshape(rows, 2, TP, UNITS).transpose(2, 0, 1, 3).reshape(TP, rows, 2 * UNITS)
    down = low[:, edge:].reshape(rows, TP, UNITS).transpose(1, 0, 2)
    return jnp.concatenate([heads, both, down, out, jnp.zeros((TP, rows, 256 - HEADS * DH), HALF)], axis=2)


def unpack_columns(grads):
    rows = grads.shape[1]
    wide = grads.astype(FULL)
    at = QKVG + 2 * UNITS
    heads = wide[:, :, :QKVG].reshape(TP, rows, HEADS, 4, DH).transpose(1, 3, 0, 2, 4).reshape(rows, 4 * D)
    out = wide[:, :, at + UNITS : at + UNITS + HEADS * DH].transpose(1, 0, 2).reshape(rows, D)
    both = wide[:, :, QKVG:at].reshape(TP, rows, 2, UNITS).transpose(1, 2, 0, 3).reshape(rows, 2 * F)
    down = wide[:, :, at : at + UNITS].transpose(1, 0, 2).reshape(rows, F)
    return jnp.concatenate([heads, out, both, down], axis=1)


def pad_lanes(value, width=LANES):
    return jnp.pad(value, ((0, 0), (0, width - value.shape[1])))


def grad_of(left, right):
    return jnp.einsum("tr,tc->rc", left, right, preferred_element_type=FULL).astype(HALF)


def shards(
    inputs,
    cotangent,
    weights,
    weights_first,
    weights_second,
    gains,
    gains_first,
    gains_second,
    forget_weight,
    forget_first,
    forget_second,
    forget_bias,
    bias_first,
    bias_second,
):
    grps, groups = lax.axis_size("grp"), lax.axis_size("fsdp") // TP
    grp, group, member = place()
    rows, own_rows = inputs.shape[1], weights.shape[0]
    group_tokens = TP * rows
    span = groups * group_tokens
    source, returned = inputs[0], cotangent[0]
    where = jnp.stack([group, jnp.int32(groups)]).astype(jnp.int32)

    low = rms_rows(source.astype(FULL), gains[0]).astype(HALF)
    tokens, returned_all, full = start(low, returned, pack_columns(weights), grps, groups)
    tokens = tokens.reshape(span, D)
    returned_all = returned_all.reshape(group_tokens, D)
    full = full.reshape(D, WIDTH)

    forget_low = pad_lanes(lax.dynamic_slice_in_dim(forget_weight, member * HEADS, HEADS, 1).astype(HALF))
    bias = pad_lanes(lax.dynamic_slice_in_dim(forget_bias[None], member * HEADS, HEADS, 1))
    head_gains = lax.dynamic_slice_in_dim(gains[2:4], member * HEADS * DH, HEADS * DH, 1)
    head_gains = head_gains.reshape(2, HEADS, DH).transpose(1, 0, 2).reshape(HEADS, 2 * DH)
    head_gains = jnp.pad(head_gains, ((0, 8 - HEADS), (0, 0)))
    queries, keys, values, made, logits, sums = project(tokens, full, forget_low, bias, head_gains)
    gated, attended, logs = attend(where, queries, keys, values, made, group_tokens)
    mixed, second = mix(gated, full, source, gains[1:2])
    second = second.reshape(group_tokens, D)
    hidden, grad_both = feed(second, returned_all, full)
    output, grad_mixed, grad_gain_mid, branch = unmix(grad_both, hidden, full, mixed, gains[1:2], returned)
    branch = branch.reshape(group_tokens, D)

    grads_low, queries_back, grad_gates, pack = ungate(where, branch, full, attended, made, logs, sums, queries)
    size = lax.axis_size("fsdp")
    others = [
        lax.ppermute(pack, "fsdp", [((at + step * TP) % size, at) for at in range(size)])
        for step in range(1, groups)
    ]
    others = jnp.concatenate(others, axis=0)
    dqueries, dkeys, dvalues = own_back(where, queries_back, grads_low, keys, values)
    dkeys, dvalues, late = later_back(where, queries, others, keys, values, dkeys, dvalues)
    later = pad_lanes(late[:, 0, DH + 3][None])
    if groups > 2:
        everyone = lax.all_gather(dkeys[:, :, DH + 3].sum(axis=1) - dqueries[:, :, DH].sum(axis=1), "fsdp")
        ahead = (jnp.arange(size) // TP > group) & (jnp.arange(size) % TP == member)
        later = pad_lanes(-jnp.sum(jnp.where(ahead[:, None], everyone, 0.0), axis=0)[None])
    grad_projected, grad_logits, grad_heads, grad_bias = unproject(
        where, dqueries, dkeys, dvalues, grad_gates, made, logits, head_gains, later
    )
    input_grad, grad_gain_in = finish(
        grad_projected, full, grad_logits, forget_low, source, gains[0:1], grad_mixed
    )

    first = lax.dynamic_slice_in_dim(tokens, group * group_tokens, group_tokens, 0)
    partial = jnp.concatenate(
        [
            grad_of(first, grad_projected),
            grad_of(second, grad_both),
            grad_of(returned_all, hidden),
            grad_of(branch, gated),
        ],
        axis=1,
    )
    mine = give_back(partial.reshape(grps, groups, TP, own_rows, WIDTH), grps, groups)

    grad_forget = jnp.einsum("th,td->hd", grad_logits[:, :HEADS], first, preferred_element_type=FULL)
    grad_heads = grad_heads[:HEADS].reshape(HEADS, 2, DH).transpose(1, 0, 2).reshape(2, HEADS * DH)
    small = jnp.zeros((32, D), FULL)
    small = lax.dynamic_update_slice(small, grad_forget, (member * HEADS, 0))
    small = lax.dynamic_update_slice(small, grad_gain_in, (H, 0))
    small = lax.dynamic_update_slice(small, grad_gain_mid, (H + 1, 0))
    small = lax.dynamic_update_slice(small, grad_heads, (H + 2, member * HEADS * DH))
    small = lax.dynamic_update_slice(small, grad_bias[0:1, :HEADS], (H + 4, member * HEADS))
    small = total_of(small, 6)
    grad_forget = small[:H].T
    grad_gains = small[H : H + 4]
    grad_bias = small[H + 4, :H]

    wide = mine.astype(FULL)
    squares = total_of(jnp.full((8, LANES), jnp.sum(wide * wide), FULL), 7)[0, 0]
    grad_norm = jnp.sqrt(squares + jnp.sum(small * small))
    factor = CLIP / jnp.maximum(grad_norm, CLIP)
    new_w, new_wf, new_ws = adam(
        weights, weights_first, weights_second, unpack_columns(mine) * factor, RATE_MATRIX, DECAY
    )
    new_g, new_gf, new_gs = adam(gains, gains_first, gains_second, grad_gains * factor, RATE_GAIN, 0.0)
    new_fw, new_ff, new_fs = adam(
        forget_weight, forget_first, forget_second, grad_forget * factor, RATE_MATRIX, DECAY
    )
    new_fb, new_bf, new_bs = adam(
        forget_bias, bias_first, bias_second, grad_bias * factor, RATE_BIAS, 0.0
    )
    return (
        output[None],
        input_grad[None],
        grad_norm,
        new_w,
        new_wf,
        new_ws,
        new_g,
        new_gf,
        new_gs,
        new_fw,
        new_ff,
        new_fs,
        new_fb,
        new_bf,
        new_bs,
    )


def solution(mesh):
    tokens = P("grp", "fsdp", None)
    matrix = P(("grp", "fsdp"), None)
    return jax.shard_map(
        shards,
        mesh=mesh,
        in_specs=(tokens,) * 2 + (matrix,) * 3 + (P(),) * 9,
        out_specs=(tokens,) * 2 + (P(),) + (matrix,) * 3 + (P(),) * 9,
        check_vma=False,
    )
```

time: 2380 us -> 688 us (0.29)
  waiting for transfers between devices: 1630 us -> 3.28 us
  Pallas kernels: 0 us -> 563 us
  matrix products: 214 us -> 14.8 us
  blocking collectives: 137 us -> 0 us
  local copies, waits for them, and re-layouts: 194 us -> 63.2 us
  other arithmetic: 146 us -> 26.4 us
    reduce_scatter x2 -> x0, waiting for transfers between devices: 1110 us -> none  [the longest x1 1060 us: shards(): lax.psum_scatter(grad_terms(pairs=attn_pairs + mlp_pairs), 'fsdp', scatte...]
    pallas_call x0 -> x14, Pallas kernels: none -> 563 us  [the longest x1 175 us: start(): pl.pallas_call(functools.partial(start_kernel, grps, groups), out_shape=(...]
    all_gather x8 -> x0, waiting for transfers between devices: 434 us -> none  [the longest x1 151 us: shards(): lax.all_gather(narrow[:, 5 * D:5 * D + 2 * F], ('grp', 'fsdp'), axis=0, t...]
    dot_general x36 -> x5, matrix products: 214 us -> 14.8 us  [the longest x4 14.3 us: grad_of(): jnp.einsum('tr,tc->rc', left, right, preferred_element_type=FULL)]
    psum x1 -> x0, waiting for transfers between devices: 83.1 us -> none  [shards(): lax.psum((jnp.sum(grad_weights * grad_weights), grad_gains, grad_forget,...]
    concatenate x1, other arithmetic: 80.2 us -> 3.81 us  [shards(): jnp.concatenate([grad_of(first, grad_projected), grad_of(second, grad_bot...]
    another operation x9 -> x0, local copies, waits for them, and re-layouts: 67.2 us -> none  [the longest x4 65.1 us: split_blocks(): return array.reshape((array.shape[0] // step, step) + array.shape[1:])]
    all_gather x3 -> x0, blocking collectives: 66.7 us -> none  [the longest x1 26.6 us: shards(): lax.all_gather(local_sum, 'fsdp', axis=0, tiled=True)]
  transfers between devices with their start and end apart: 11 -> 1, of which waited for: 10 -> 1; matrix products, arithmetic and copies ran while one was open for 12% -> 1% of each run, Pallas kernels for 0% -> 2%
where the time goes in v1:
time: 688 us; the launch traced here: 684 us
  Pallas kernels  563 us (82%)
  local copies, waits for them, and re-layouts  63.2 us (9%)
  other arithmetic  26.4 us (4%)
  matrix products  14.8 us (2%)
  starting transfers between devices  9.28 us (1%)
    pallas_call x1, Pallas kernels, start(): pl.pallas_call(functools.partial(start_kernel, grps, groups), out_shape=(...  175 us
    pallas_call x1, Pallas kernels, give_back(): pl.pallas_call(functools.partial(return_kernel, grps, groups), out_shape=...  116 us
    pallas_call x1, Pallas kernels, unmix(): pl.pallas_call(unmix_kernel, grid=(1,), out_shape=(jax.ShapeDtypeStruct((...  65.4 us
    pallas_call x2, Pallas kernels, total_of(): pl.pallas_call(functools.partial(total_kernel, tuple(bits)), out_shape=ja...  46.7 us
    pallas_call x1, Pallas kernels, mix(): pl.pallas_call(mix_kernel, grid=(1,), out_shape=(jax.ShapeDtypeStruct((ro...  46.5 us
    pallas_call x1, Pallas kernels, finish(): pl.pallas_call(finish_kernel, grid=(1,), out_shape=(jax.ShapeDtypeStruct(...  28.9 us
    pallas_call x1, Pallas kernels, project(): pl.pallas_call(project_kernel, grid=(tokens // ROWS,), out_shape=(jax.Sha...  19.8 us
    pallas_call x1, Pallas kernels, later_back(): pl.pallas_call(later_kernel, grid_spec=pltpu.PrefetchScalarGridSpec(num_s...  16.5 us
  transfers between devices with their start and end apart: 1, of which 1 were waited for; matrix products, arithmetic and copies ran while one was open for 1% of the time, Pallas kernels for 2%

profile of v1, /device:TPU:0, one launch (start us, length us, event | category | flops | bytes accessed | tf_op | source)
XLA Modules:
  0.0 684.0 jit_solution(9422536401344241422)
XLA Ops:
  0.6 1.3 slice.72
  2.0 1.4 fusion.21
  3.4 2.3 convert_element_type.37
  6.3 0.7 copy.61
  7.9 1.4 reshape.125
  9.3 1.6 reshape.122
  10.9 0.9 copy.36
  11.9 0.7 reshape.123
  12.6 0.9 fusion.6.a_ref
  13.5 3.6 concatenate.9.w_ref
  17.1 174.6 %start.1 = (bf16[2,8,128,1536]{3,2,1,0:T(8,128)(2,1)}, bf16[8,128,1536]{2,1,0:T(8,128)(2,1)}, bf16[2,2,8,48,2560]{4,3,2,1,0:T(8,128)(2,1)}) custom-call(bf16[128,1536]{1,0:T(8,128)(2,1)} %fusion.6.a_ref, bf16[128,1536]{1,0:T(8,128)(2,1)} %bitcast.109, bf16[8,48,2560]{2,1,0:T(8,128)(2,1)} %concatenate.9.w_ref), custom_call_target="tpu_custom_call" | custom-call | tf_op jit(solution)/shard_map/start/pallas_call | solution.py:216
  191.7 2.7 slice.93.wd_ref
  194.3 3.9 slice.92.wgu_ref
  198.3 0.9 constant_dynamic-slice_fusion.1
  199.2 0.8 constant_dynamic-slice_fusion
  201.5 0.8 pad.15.f_ref
  202.9 19.8 %project.1 = (bf16[3,2048,128]{2,1,0:T(8,128)(2,1)}, bf16[3,2048,128]{2,1,0:T(8,128)(2,1)}, bf16[3,2048,128]{2,1,0:T(8,128)(2,1)}, f32[2048,768]{1,0:T(8,128)}, ...) custom-call(bf16[2048,1536]{1,0:T(8,128)(2,1)} %bitcast.84, bf16[1536,2560]{1,0:T(8,128)(2,1)} %bitcast.79, ...), custom_call_target="tpu_custom_call" | custom-call | tf_op jit(solution)/shard_map/project/pallas_call | solution.py:310
  222.7 10.2 %attend.1 = (bf16[1024,256]{1,0:T(8,128)(2,1)}, f32[1024,256]{1,0:T(8,128)}, f32[1024,128]{1,0:T(8,128)}) custom-call(s32[2]{0:T(128)} %pad_add_fusion.where_ref, bf16[3,2048,128]{2,1,0:T(8,128)(2,1)} %get-tuple-element.53.q_ref, bf16[3,2048,128]{2,1,0:T(8,128)(2,1)} %get-tuple-element.54.k_ref, bf16[3,2048,128]{2,1,0:T(8,128)(2,1)} %get-tuple-element.55.v_ref, ...), custom_call_target="tpu_custom_call" | custom-call | tf_op jit(solution)/shard_map/attend/pallas_call | solution.py:402
  232.9 46.5 %mix.1 = (f32[128,1536]{1,0:T(8,128)}, bf16[8,128,1536]{2,1,0:T(8,128)(2,1)}) custom-call(bf16[4,2,128,256]{3,2,1,0:T(8,128)(2,1)} %bitcast.117, bf16[1536,2560]{1,0:T(8,128)(2,1)} %bitcast.80, bf16[128,1536]{1,0:T(8,128)(2,1)} %bitcast.92, f32[1,1536]{1,0:T(1,128)} %get-tuple-element.101.g_ref), custom_call_target="tpu_custom_call" | custom-call | tf_op jit(solution)/shard_map/mix/pallas_call | solution.py:533
  279.4 10.3 %feed.1 = (bf16[1024,512]{1,0:T(8,128)(2,1)}, bf16[1024,1024]{1,0:T(8,128)(2,1)}) custom-call(bf16[1024,1536]{1,0:T(8,128)(2,1)} %bitcast.106, bf16[1024,1536]{1,0:T(8,128)(2,1)} %bitcast.104, bf16[1536,1024]{1,0:T(8,128)(2,1)} %slice.92.wgu_ref, bf16[1536,512]{1,0:T(8,128)(2,1)} %slice.93.wd_ref), custom_call_target="tpu_custom_call" | custom-call | tf_op jit(solution)/shard_map/feed/pallas_call | solution.py:697
  289.7 65.4 %unmix.1 = (bf16[128,1536]{1,0:T(8,128)(2,1)}, f32[128,1536]{1,0:T(8,128)}, f32[1,1536]{1,0:T(1,128)}, bf16[8,128,1536]{2,1,0:T(8,128)(2,1)}) custom-call(bf16[4,2,128,1024]{3,2,1,0:T(8,128)(2,1)} %bitcast.108, bf16[1536,1024]{1,0:T(8,128)(2,1)} %slice.92.wgu_ref, bf16[4,2,128,512]{3,2,1,0:T(8,128)(2,1)} %bitcast.114, bf16[1536,512]{1,0:T(8,128)(2,1)} %slice.93.wd_ref, ...), custom_call_target="tpu_custom_call" | custom-call | tf_op jit(solution)/shard_map/unmix/pallas_call | solution.py:589
  355.1 8.9 %ungate.1 = (bf16[3,1024,128]{2,1,0:T(8,128)(2,1)}, bf16[3,1024,128]{2,1,0:T(8,128)(2,1)}, f32[1024,256]{1,0:T(8,128)}, bf16[1024,256]{1,0:T(8,128)(2,1)}) custom-call(s32[2]{0:T(128)} %pad_add_fusion.where_ref, bf16[1024,1536]{1,0:T(8,128)(2,1)} %bitcast.99, bf16[1536,2560]{1,0:T(8,128)(2,1)} %bitcast.81, f32[1024,256]{1,0:T(8,128)} %get-tuple-element.65.o_ref, ...), custom_call_target="tpu_custom_call" | custom-call | tf_op jit(solution)/shard_map/ungate/pallas_call | solution.py:765
  364.0 9.3 %collective-permute-start = (bf16[1024,256]{1,0:T(8,128)(2,1)}, bf16[1024,256]{1,0:T(8,128)(2,1)}, u32[]{:S(2)}, u32[]{:S(2)}) collective-permute-start(bf16[1024,256]{1,0:T(8,128)(2,1)} %get-tuple-element.71), channel_id=1, source_target_pairs={{8,0},{9,1},{10,2},{11,3},{12,4},{13,5},{14,6},{15,7},{0,8},{1,9},... | collective-permute-start | bytes 1572872 | tf_op jit(solution)/shard_map/ppermute | solution.py:1232
  373.3 4.9 convolution_convert_fusion
  378.2 1.9 convolution_convert_fusion.3
  380.1 11.2 %own_back.1 = (f32[3,1024,128]{2,1,0:T(8,128)}, f32[3,1024,128]{2,1,0:T(8,128)}, f32[3,1024,128]{2,1,0:T(8,128)}) custom-call(s32[2]{0:T(128)} %pad_add_fusion.where_ref, bf16[3,1024,128]{2,1,0:T(8,128)(2,1)} %get-tuple-element.68.q_ref, bf16[3,1024,128]{2,1,0:T(8,128)(2,1)} %get-tuple-element.69.do_ref, bf16[3,2048,128]{2,1,0:T(8,128)(2,1)} %get-tuple-element.54.k_ref, ...), custom_call_target="tpu_custom_call" | custom-call | tf_op jit(solution)/shard_map/own_back/pallas_call | solution.py:843
  391.3 3.0 convolution_convert_fusion.2
  394.3 3.3 collective-permute-done.pack_ref
  397.6 16.5 %later_back.1 = (f32[3,1024,128]{2,1,0:T(8,128)}, f32[3,1024,128]{2,1,0:T(8,128)}, f32[3,8,128]{2,1,0:T(8,128)}) custom-call(s32[2]{0:T(128)} %pad_add_fusion.where_ref, bf16[3,2048,128]{2,1,0:T(8,128)(2,1)} %get-tuple-element.53.q_ref, bf16[1024,256]{1,0:T(8,128)(2,1)} %collective-permute-done.pack_ref, bf16[3,2048,128]{2,1,0:T(8,128)(2,1)} %get-tuple-element.54.k_ref, ...), custom_call_target="tpu_custom_call" | custom-call | tf_op jit(solution)/shard_map/later_back/pallas_call | solution.py:896
  414.2 0.9 slice_reduce_fusion
  415.6 8.5 %unproject.1 = (bf16[1024,768]{1,0:T(8,128)(2,1)}, bf16[1024,128]{1,0:T(8,128)(2,1)}, f32[8,128]{1,0:T(8,128)}, f32[8,128]{1,0:T(8,128)}) custom-call(s32[2]{0:T(128)} %pad_add_fusion.where_ref, f32[3,1024,128]{2,1,0:T(8,128)} %get-tuple-element.70.dq_ref, f32[3,1024,128]{2,1,0:T(8,128)} %get-tuple-element.74.dk_ref, ...), custom_call_target="tpu_custom_call" | custom-call | tf_op jit(solution)/shard_map/unproject/pallas_call | solution.py:975
  424.2 4.5 convolution_convert_fusion.1
  428.7 3.8 pad_maximum_fusion
  432.5 10.8 %copy.42 = bf16[1536,2560]{1,0:T(8,128)(2,1)} copy(bf16[1536,2560]{0,1:T(8,128)(2,1)} %pad_maximum_fusion) | data formatting | bytes 15728640 | tf_op jit(solution)/shard_map/concatenate | solution.py:1251
  443.4 115.6 %give_back.1 = bf16[8,48,2560]{2,1,0:T(8,128)(2,1)} custom-call(bf16[2,2,8,48,2560]{4,3,2,1,0:T(8,128)(2,1)} %bitcast.83), custom_call_target="tpu_custom_call" | custom-call | tf_op jit(solution)/shard_map/give_back/pallas_call | solution.py:1082
  559.0 3.3 multiply_reduce_fusion
  562.3 1.2 slice.94
  563.5 1.3 slice.96
  565.3 0.8 slice_bitcast_fusion.1
  566.1 0.9 slice_bitcast_fusion
  567.8 28.9 %finish.1 = (bf16[128,1536]{1,0:T(8,128)(2,1)}, f32[1,1536]{1,0:T(1,128)}) custom-call(bf16[4,2,128,768]{3,2,1,0:T(8,128)(2,1)} %bitcast.112, bf16[1536,2560]{1,0:T(8,128)(2,1)} %bitcast.82, bf16[4,2,128,128]{3,2,1,0:T(8,128)(2,1)} %bitcast.115, bf16[1536,128]{1,0:T(8,128)(2,1)} %pad.15.f_ref, bf16[128,1536]{1,0:T(8,128)(2,1)} %bitcast.93, ...), custom_call_target="tpu_custom_call" | custom-call | tf_op jit(solution)/shard_map/finish/pallas_call | solution.py:651
  596.8 0.7 slice.80
  598.0 0.8 dynamic_update_slice.16
  599.1 0.7 dynamic_update_slice.18
  600.0 0.7 copy-done.13
  600.7 34.4 %total_of.3 = f32[32,1536]{1,0:T(8,128)} custom-call(f32[32,1536]{1,0:T(8,128)} %copy-done.13), custom_call_target="tpu_custom_call" | custom-call | tf_op jit(solution)/shard_map/total_of/pallas_call | solution.py:1131
  635.0 1.6 multiply_reduce_fusion.1
  636.6 1.2 broadcast_in_dim.20.value_ref
  637.9 12.3 %total_of.2 = f32[8,128]{1,0:T(8,128)} custom-call(f32[8,128]{1,0:T(8,128)} %broadcast_in_dim.20.value_ref), custom_call_target="tpu_custom_call" | custom-call | tf_op jit(solution)/shard_map/total_of/pallas_call | solution.py:1131
  650.2 1.2 slice.77
  652.7 2.4 reshape.143
  655.1 2.5 copy.58
  657.7 2.7 reshape.144
  660.4 2.6 reshape.146
  663.1 0.9 copy.46
  664.0 0.9 copy.52
  665.0 1.0 copy.45
  666.0 1.8 reshape.145
  667.9 1.2 multiply_subtract_fusion.3
  669.1 1.5 multiply_subtract_fusion.2
  670.5 1.9 multiply_subtract_fusion.1
  672.5 8.6 %multiply_subtract_fusion = (f32[48,19968]{1,0:T(8,128)}, f32[48,19968]{1,0:T(8,128)}, f32[48,19968]{1,0:T(8,128)}) fusion(f32[48,19968]{1,0:T(8,128)} %param.16, f32[]{:T(128)S(6)} %div.84, f32[48,4096]{1,0:T(8,128)S(1)} %bitcast.98, f32[48,8192]{1,0:T(8,128)S(1)} %bitcast.94, f32[48,1536]{1,0:T(8,128)} %reshape.145, f32[48,6144]{1,0:T(8,128)S(1)} %copy-done.2, ...), kind=kLoop, calls=%fused_computation.5 | loop fusion | flops 18210816 | bytes 26836996 | tf_op jit(solution)/shard_map/sub | solution.py:1152
  681.1 0.7 copy.70
  681.9 0.7 copy.71
  (86 shorter events, 6.5 us)
Async XLA Ops:
  3.4 2.5 copy-start.1
  194.3 3.9 copy-start.20
  355.1 18.2 %copy-start.6 = (bf16[8,128,1536]{2,1,0:T(8,128)(2,1)S(1)}, bf16[8,128,1536]{2,1,0:T(8,128)(2,1)}, u32[]{:S(2)}) copy-start(bf16[8,128,1536]{2,1,0:T(8,128)(2,1)} %get-tuple-element.58) | copy-start | bytes 9437188
  355.1 18.2 %copy-start.8 = (bf16[1024,1024]{1,0:T(8,128)(2,1)S(1)}, bf16[1024,1024]{1,0:T(8,128)(2,1)}, u32[]{:S(2)}) copy-start(bf16[1024,1024]{1,0:T(8,128)(2,1)} %get-tuple-element.60) | copy-start | bytes 6291460
  364.0 14.2 %copy-start.3 = (bf16[8,128,1536]{2,1,0:T(8,128)(2,1)S(1)}, bf16[8,128,1536]{2,1,0:T(8,128)(2,1)}, u32[]{:S(2)}) copy-start(bf16[8,128,1536]{2,1,0:T(8,128)(2,1)} %get-tuple-element.64) | copy-start | bytes 9437188
  364.0 14.1 %copy-start.15 = (bf16[1024,256]{1,0:T(8,128)(2,1)S(1)}, bf16[1024,256]{1,0:T(8,128)(2,1)}, u32[]{:S(2)}) copy-start(bf16[1024,256]{1,0:T(8,128)(2,1)} %get-tuple-element.57) | copy-start | bytes 1572868
  364.0 33.6 %collective-permute-start = (bf16[1024,256]{1,0:T(8,128)(2,1)}, bf16[1024,256]{1,0:T(8,128)(2,1)}, u32[]{:S(2)}, u32[]{:S(2)}) collective-permute-start(bf16[1024,256]{1,0:T(8,128)(2,1)} %get-tuple-element.71), channel_id=1, source_target_pairs={{8,0},{9,1},{10,2},{11,3},{12,4},{13,5},{14,6},{15,7},{0,8},{1,9},... | collective-permute-start | bytes 1572872 | tf_op jit(solution)/shard_map/ppermute | solution.py:1232
  380.1 11.2 %copy-start.5 = (bf16[8,128,1536]{2,1,0:T(8,128)(2,1)S(1)}, bf16[8,128,1536]{2,1,0:T(8,128)(2,1)}, u32[]{:S(2)}) copy-start(bf16[8,128,1536]{2,1,0:T(8,128)(2,1)} %get-tuple-element.59) | copy-start | bytes 9437188
  380.1 11.2 %copy-start.11 = (bf16[1024,512]{1,0:T(8,128)(2,1)S(1)}, bf16[1024,512]{1,0:T(8,128)(2,1)}, u32[]{:S(2)}) copy-start(bf16[1024,512]{1,0:T(8,128)(2,1)} %get-tuple-element.61) | copy-start | bytes 3145732
  397.6 26.5 %slice-start = ((s8[6291456]{0:T(1024)(128)(4,1)}), s8[4194304]{0:T(1024)(128)(4,1)S(1)}, s32[]{:S(2)}) async-start(s8[6291456]{0:T(1024)(128)(4,1)} %bitcast.85), calls=%async_computation | async-start | bytes 8388608
  415.6 8.5 %slice-start.1 = ((s8[6291456]{0:T(1024)(128)(4,1)}), s8[2097152]{0:T(1024)(128)(4,1)S(1)}, s32[]{:S(2)}) async-start(s8[6291456]{0:T(1024)(128)(4,1)} %bitcast.85), calls=%async_computation.1 | async-start | bytes 4194304
  424.1 4.6 copy-start.7
  424.1 4.6 copy-start.10
  424.2 4.6 copy-start.14
  559.0 4.5 copy-start
  563.5 3.6 slice-start.2
  564.9 2.4 slice-start.3
  564.9 2.4 copy-start.12
  567.8 28.9 %copy-start.19 = (f32[8,128]{1,0:T(8,128)S(1)}, f32[8,128]{1,0:T(8,128)}, u32[]{:S(2)}) copy-start(f32[8,128]{1,0:T(8,128)} %get-tuple-element.85) | copy-start | bytes 12292
  567.8 31.1 %copy-start.18 = (f32[1,1536]{1,0:T(1,128)S(1)}, f32[1,1536]{1,0:T(1,128)}, u32[]{:S(2)}) copy-start(f32[1,1536]{1,0:T(1,128)} %get-tuple-element.84) | copy-start | bytes 18436
  600.0 0.7 copy-start.13
  663.0 1.9 copy-start.4
  663.1 2.0 copy-start.9
  664.0 3.9 copy-start.21
  664.0 3.9 copy-start.22
  664.0 8.5 %copy-start.2 = (f32[48,6144]{1,0:T(8,128)S(1)}, f32[48,6144]{1,0:T(8,128)}, u32[]{:S(2)}) copy-start(f32[48,6144]{1,0:T(8,128)} %reshape.144) | copy-start | bytes 3538948
  672.5 8.6 %copy-start.16 = (bf16[128,1536]{1,0:T(8,128)(2,1)S(1)}, bf16[128,1536]{1,0:T(8,128)(2,1)}, u32[]{:S(2)}) copy-start(bf16[128,1536]{1,0:T(8,128)(2,1)} %get-tuple-element.63) | copy-start | bytes 1179652
  672.5 9.4 %copy-start.17 = (bf16[128,1536]{1,0:T(8,128)(2,1)S(1)}, bf16[128,1536]{1,0:T(8,128)(2,1)}, u32[]{:S(2)}) copy-start(bf16[128,1536]{1,0:T(8,128)(2,1)} %get-tuple-element.82) | copy-start | bytes 1179652
